TPU v7x, 32 devices: a whole 2x2x4 slice. The times are simulated.
32 devices in a mesh: expert: 4 (over y, x), dp: 8 (over z, core).
Axes of the slice: x: 2, y: 2, z: 4, core: 2. Of those that a mesh axis runs over, the one named last changes fastest.
Arguments:
- tokens: bfloat16 [1024, 7168], P('dp', 'expert'), may hold values from -6 to 6
- grad_out: bfloat16 [1024, 7168], P('dp', 'expert'), may hold values from -6 to 6
- expert_ids: int32 [1024, 2], P('dp'), may hold values from -1 to 3, as said below
- route_weights: float32 [1024, 2], P('dp'), may hold values from 0.1 to 1
- w_gate: bfloat16 [4, 7168, 2048], P('expert', 'dp'), may hold values from -0.0625 to 0.0625
- w_up: bfloat16 [4, 7168, 2048], P('expert', 'dp'), may hold values from -0.0625 to 0.0625
- w_down: bfloat16 [4, 2048, 7168], P('expert', None, 'dp'), may hold values from -0.125 to 0.125
Outputs:
- grad_tokens: bfloat16 [1024, 7168], P('dp', 'expert')
- grad_gate: bfloat16 [4, 7168, 2048], P('expert', 'dp')
- grad_up: bfloat16 [4, 7168, 2048], P('expert', 'dp')
- grad_down: bfloat16 [4, 2048, 7168], P('expert', None, 'dp')
Inputs may be any that keep to these rules, and one draw needn't show every extreme that they name: expert_ids[t, 0] is an expert; expert_ids[t, 1] is another expert or -1. Within each block of 128 rows (the tokens of one index of dp) no expert appears in more than 64 rows, and one expert, the same in every block, appears in exactly 64 rows, each of which has -1 as its second entry.
All inputs are finite; a program needn't handle non-finite values.
Results may differ from a plain program's by a relative error of at most 0.03.
Values may be sent and summed in bfloat16 or wider, within the bound.
No kernel may reach another device: no remote copies, remote signals or barrier semaphores. Data moves between devices by JAX's collectives and lax.ppermute only.
A program may use at most 128 MiB of HBM per device.

v0:
```python
import functools
import math

import jax
import jax.numpy as jnp
from jax import lax
from jax.experimental import pallas as pl
from jax.experimental.pallas import tpu as pltpu
from jax.sharding import PartitionSpec as P

F32 = jnp.float32
BF16 = jnp.bfloat16
LAST_DIMS = (((1,), (1,)), ((), ()))
ROWS_FIRST = (((0,), (0,)), ((), ()))
FIXED = 5
PARTS = 2
PARAMS = pltpu.CompilerParams(vmem_limit_bytes=28 * 1024 * 1024)


def dot(a, b, dims=None):
    if dims is None:
        return jnp.dot(a, b, preferred_element_type=F32)
    return lax.dot_general(a, b, dims, preferred_element_type=F32)


def cost():
    return pl.CostEstimate(flops=1024, bytes_accessed=1024, transcendentals=0)


def in_hbm(*arrays):
    return [pltpu.with_memory_space_constraint(a, pltpu.HBM) for a in arrays]


def pass_on(scalar_ref, out_ref):
    for n in range(out_ref.shape[0]):
        out_ref[n] = scalar_ref[n]


def slot_one_hot(ids_ref, experts, capacity):
    tokens = ids_ref.shape[1]
    first, second = ids_ref[0:1, :], ids_ref[1:2, :]
    expert = lax.broadcasted_iota(jnp.int32, (8 * (-(-experts // 8)), tokens), 0)
    chosen = (first == expert) | (second == expert)
    before = lax.broadcasted_iota(jnp.int32, (tokens, tokens), 0) < lax.broadcasted_iota(
        jnp.int32, (tokens, tokens), 1
    )
    place = dot(chosen.astype(F32).astype(BF16), before.astype(F32).astype(BF16))
    place = jnp.where(chosen, place, -1.0).astype(jnp.int32)
    slot = lax.broadcasted_iota(jnp.int32, (capacity, tokens), 0)
    return [slot == place[e : e + 1, :] for e in range(experts)]


def dispatch_kernel(experts, weighted, scalar_ref, ids_hbm, weights_hbm, rows_hbm, *refs):
    *messages, hot_ref, token_ref, ids_ref, weights_ref, rows_ref, scale_ref, sems = refs
    _, capacity, feats = messages[0].shape
    pass_on(scalar_ref, token_ref)
    pairs = [(ids_hbm, ids_ref), (weights_hbm, weights_ref)]
    for h in range(2):
        whole = len(rows_hbm.shape) == 3
        half = rows_hbm.at[h] if whole else rows_hbm.at[:, pl.ds(h * feats, feats)]
        pairs.append((half, rows_ref.at[h]))
    copies = [pltpu.make_async_copy(a, b, sems.at[n]) for n, (a, b) in enumerate(pairs)]
    for copy in copies:
        copy.start()
    copies[0].wait()
    copies[1].wait()
    for e, hit in enumerate(slot_one_hot(ids_ref, experts, capacity)):
        place = slice(e * capacity, (e + 1) * capacity)
        hot_ref[place, :] = hit.astype(F32).astype(BF16)
        if weighted:
            weight = jnp.where(ids_ref[0:1, :] == e, weights_ref[0:1, :], weights_ref[1:2, :])
            weight = jnp.sum(jnp.where(hit, weight, 0.0), axis=1, keepdims=True)
            scale_ref[place, :] = jnp.broadcast_to(weight, (capacity, scale_ref.shape[1]))
    places = [
        pl.ds(pl.multiple_of((scalar_ref[4] ^ t) * capacity, capacity), capacity)
        for t in range(experts)
    ]
    hot = jnp.concatenate([hot_ref[place, :] for place in places], axis=0)
    for h in range(2):
        copies[2 + h].wait()
        out = dot(hot, rows_ref[h])
        for t, place in enumerate(places):
            part = out[t * capacity : (t + 1) * capacity]
            if weighted:
                part = part * scale_ref[place, 0:1]
            messages[t][h] = part.astype(BF16)


def dispatch_rows(scalars, ids, weights, rows, experts, weighted):
    tokens, feats = rows.shape[0], rows.shape[1] // 2
    capacity = tokens // 2
    if feats % 128:
        rows = rows.reshape(tokens, 2, feats).transpose(1, 0, 2)
    *messages, hot, token = pl.pallas_call(
        functools.partial(dispatch_kernel, experts, weighted),
        out_shape=[jax.ShapeDtypeStruct((2, capacity, feats), BF16)] * experts
        + [
            jax.ShapeDtypeStruct((experts * capacity, tokens), BF16),
            jax.ShapeDtypeStruct(scalars.shape, jnp.int32),
        ],
        in_specs=[pl.BlockSpec(memory_space=pltpu.SMEM)]
        + [pl.BlockSpec(memory_space=pltpu.HBM)] * 3,
        out_specs=[pl.BlockSpec(memory_space=pltpu.VMEM)] * (experts + 1)
        + [pl.BlockSpec(memory_space=pltpu.SMEM)],
        scratch_shapes=[
            pltpu.VMEM((2, tokens), jnp.int32),
            pltpu.VMEM((2, tokens), F32),
            pltpu.VMEM((2, tokens, feats), BF16),
            pltpu.VMEM((experts * capacity, 128), F32),
            pltpu.SemaphoreType.DMA((4,)),
        ],
        compiler_params=PARAMS,
        cost_estimate=cost(),
    )(scalars, *in_hbm(ids, weights, rows))
    return messages, hot, token


def assemble_kernel(scalar_ref, *refs):
    *messages, out_ref, token_ref, sems = refs
    pass_on(scalar_ref, token_ref)

    def copy(t, message):
        return pltpu.make_async_copy(message, out_ref.at[t ^ scalar_ref[4]], sems.at[t])

    for t, message in enumerate(messages):
        copy(t, message).start()
    for t, message in enumerate(messages):
        copy(t, message).wait()


def assemble(scalars, messages):
    return pl.pallas_call(
        assemble_kernel,
        out_shape=(
            jax.ShapeDtypeStruct((len(messages), *messages[0].shape), BF16),
            jax.ShapeDtypeStruct(scalars.shape, jnp.int32),
        ),
        in_specs=[pl.BlockSpec(memory_space=pltpu.SMEM)]
        + [pl.BlockSpec(memory_space=pl.ANY)] * len(messages),
        out_specs=(pl.BlockSpec(memory_space=pltpu.VMEM), pl.BlockSpec(memory_space=pltpu.SMEM)),
        scratch_shapes=[pltpu.SemaphoreType.DMA((len(messages),))],
        compiler_params=PARAMS,
        cost_estimate=cost(),
    )(scalars, *messages)


def combine_kernel(experts, scalar_ref, hot_ref, *refs):
    pieces, (out_ref, rows_ref, sems) = refs[:-3], refs[-3:]
    capacity = pieces[0].shape[0]
    at = pl.program_id(0)

    def copy(n):
        return pltpu.make_async_copy(
            pieces[n], rows_ref.at[pl.ds(n * capacity, capacity)], sems.at[n]
        )

    @pl.when(at == 0)
    def _():
        for n in range(len(pieces)):
            copy(n).start()

    hot = jnp.concatenate(
        [
            hot_ref[pl.ds(pl.multiple_of((scalar_ref[2] ^ n) * capacity, capacity), capacity), :]
            for n in range(experts)
        ],
        axis=0,
    )
    for half in range(2):

        @pl.when(at == half)
        def _():
            for n in range(half * experts, (half + 1) * experts):
                copy(n).wait()
            rows = rows_ref[half * experts * capacity : (half + 1) * experts * capacity, :]
            out = dot(hot, rows, ROWS_FIRST).astype(BF16)
            out_ref[...] = out.reshape(out_ref.shape)


def combine_rows(scalars, hot, pieces, experts):
    tokens = hot.shape[1]
    capacity, feats = pieces[0].shape
    if feats % 128:
        out_shape = jax.ShapeDtypeStruct((2, tokens, feats), BF16)
        out_spec = pl.BlockSpec((1, tokens, feats), lambda a, c: (a ^ c[3], 0, 0))
    else:
        out_shape = jax.ShapeDtypeStruct((tokens, 2 * feats), BF16)
        out_spec = pl.BlockSpec((tokens, feats), lambda a, c: (0, a ^ c[3]))
    out = pl.pallas_call(
        functools.partial(combine_kernel, experts),
        out_shape=out_shape,
        grid_spec=pltpu.PrefetchScalarGridSpec(
            num_scalar_prefetch=1,
            grid=(2,),
            in_specs=[pl.BlockSpec((experts * capacity, tokens), lambda a, c: (0, 0))]
            + [pl.BlockSpec(memory_space=pltpu.HBM)] * len(pieces),
            out_specs=out_spec,
            scratch_shapes=[
                pltpu.VMEM((len(pieces) * capacity, feats), BF16),
                pltpu.SemaphoreType.DMA((len(pieces),)),
            ],
        ),
        compiler_params=PARAMS,
        cost_estimate=cost(),
    )(scalars, hot, *in_hbm(*pieces))
    if feats % 128:
        out = out.transpose(1, 0, 2).reshape(tokens, 2 * feats)
    return out


def gate_up_kernel(own, scalar_ref, x_ref, wg_ref, wu_ref, *refs):
    width = wg_ref.shape[1]
    gate = dot(x_ref[...], wg_ref[...])
    upper = dot(x_ref[...], wu_ref[...])
    *refs, token_ref = refs
    pass_on(scalar_ref, token_ref)
    if own:
        sib_ref, out_ref = refs
        gate += sib_ref[0, :, :width].astype(F32)
        upper += sib_ref[0, :, width:].astype(F32)
    else:
        out_ref, turned_ref = refs

        @pl.when(pl.program_id(0) == 0)
        def _():
            turned_ref[...] = x_ref[...].T

    out_ref[0, :, :width] = gate.astype(BF16)
    out_ref[0, :, width:] = upper.astype(BF16)


def gate_up(scalars, x, w_gate, w_up, count, sib):
    slots, feats = x.shape
    width = w_gate.shape[1] // (2 * count)
    own = sib is not None
    chunk_spec = pl.BlockSpec((1, slots, 2 * width), lambda i, c: (i, 0, 0))
    column = pl.BlockSpec(
        (feats, width), lambda i, c: (0, c[FIXED + 2 * count + own * count + i])
    )
    out_shape = [jax.ShapeDtypeStruct((count, slots, 2 * width), BF16)]
    out_specs = [chunk_spec]
    if not own:
        out_shape.append(jax.ShapeDtypeStruct((feats, slots), BF16))
        out_specs.append(pl.BlockSpec((feats, slots), lambda i, c: (0, 0)))
    out_shape.append(jax.ShapeDtypeStruct(scalars.shape, jnp.int32))
    out_specs.append(pl.BlockSpec(memory_space=pltpu.SMEM))
    return pl.pallas_call(
        functools.partial(gate_up_kernel, own),
        out_shape=out_shape,
        grid_spec=pltpu.PrefetchScalarGridSpec(
            num_scalar_prefetch=1,
            grid=(count,),
            in_specs=[pl.BlockSpec((slots, feats), lambda i, c: (0, 0)), column, column]
            + [chunk_spec] * own,
            out_specs=out_specs,
        ),
        compiler_params=PARAMS,
        cost_estimate=cost(),
    )(scalars, x, *in_hbm(w_gate, w_up), *([sib] if own else []))


def back_kernel(own, scalar_ref, g_ref, wd_ref, *refs):
    back = dot(g_ref[...], wd_ref[...], LAST_DIMS)
    if own:
        back += refs[0][0].astype(F32)
    refs[-1][0] = back.astype(BF16)


def back_rows(scalars, g, w_down, begin, size, count, sib):
    slots, feats = g.shape
    width = w_down.shape[0] // (2 * count)
    own = sib is not None
    chunk_spec = pl.BlockSpec((1, slots, width), lambda i, c: (i, 0, 0))
    row = pl.BlockSpec(
        (width, feats), lambda i, c: (c[FIXED + 2 * count + own * count + begin + i], 0)
    )
    return pl.pallas_call(
        functools.partial(back_kernel, own),
        out_shape=jax.ShapeDtypeStruct((size, slots, width), BF16),
        grid_spec=pltpu.PrefetchScalarGridSpec(
            num_scalar_prefetch=1,
            grid=(size,),
            in_specs=[pl.BlockSpec((slots, feats), lambda i, c: (0, 0)), row]
            + [chunk_spec] * own,
            out_specs=chunk_spec,
        ),
        compiler_params=PARAMS,
        cost_estimate=cost(),
    )(scalars, g, *in_hbm(w_down), *([sib] if own else []))


def activate(gate, upper, back):
    sig = jax.nn.sigmoid(gate)
    gated = gate * sig
    return (
        (gated * upper).astype(BF16),
        (back * upper * sig * (1.0 + gate * (1.0 - sig))).astype(BF16),
        (back * gated).astype(BF16),
    )


def hop_kernel(plan, scalar_ref, *refs):
    slot, count, chips, came = plan
    gate_up_ref, back_ref = refs[-3:-1]
    recv_ref = refs[0] if came else None
    send_ref = refs[-1]
    at = scalar_ref[0]
    width = send_ref.shape[1] // 3
    summing = (at <= slot) & (slot - at < count)

    def total(part):
        columns = slice(part * width, (part + 1) * width)
        value = (gate_up_ref[0, :, columns] if part < 2 else back_ref[0]).astype(F32)
        if came:
            value += jnp.where(at > 0, recv_ref[:, columns].astype(F32), 0.0)
        return value

    @pl.when(summing & (at < chips - 1))
    def _():
        for part in range(3):
            send_ref[:, part * width : (part + 1) * width] = total(part).astype(BF16)

    @pl.when(summing & (at == chips - 1))
    def _():
        for part, value in enumerate(activate(total(0), total(1), total(2))):
            send_ref[:, part * width : (part + 1) * width] = value

    if came:

        @pl.when(jnp.logical_not(summing))
        def _():
            send_ref[...] = recv_ref[...]


def hop(scalars, slot, count, chips, recv, sums, part):
    rows = sums[0][0].shape[1] // PARTS
    cols = sums[0][0].shape[2] + sums[1][0].shape[2]
    message = pl.BlockSpec((rows, cols), lambda n, c: (0, 0))
    operands, in_specs = [], []
    if recv is not None:
        operands.append(recv)
        in_specs.append(message)
    for array, i in sums:
        operands.append(array)
        in_specs.append(
            pl.BlockSpec((1, rows, array.shape[2]), lambda n, c, i=i: (i, part, 0))
        )
    plan = (slot, count, chips, recv is not None)
    return pl.pallas_call(
        functools.partial(hop_kernel, plan),
        out_shape=jax.ShapeDtypeStruct((rows, cols), BF16),
        grid_spec=pltpu.PrefetchScalarGridSpec(
            num_scalar_prefetch=1,
            grid=(1,),
            in_specs=in_specs,
            out_specs=message,
        ),
        compiler_params=PARAMS,
        cost_estimate=cost(),
    )(scalars, *operands)


def choose_kernel(wanted, hops, scalar_ref, *refs):
    *candidates, sems = refs
    candidates, outs = candidates[:-wanted], candidates[-wanted:]
    rows = candidates[0].shape[0]

    def copy(k, n, part):
        return pltpu.make_async_copy(
            candidates[(k + n) * PARTS + part],
            outs[k].at[pl.ds(part * rows, rows)],
            sems.at[k, part],
        )

    for n in range(hops):

        @pl.when(scalar_ref[0] == n)
        def _():
            for k in range(wanted):
                for part in range(PARTS):
                    copy(k, n, part).start()

    for k in range(wanted):
        for part in range(PARTS):
            copy(k, 0, part).wait()


def choose(place, wanted, hops, candidates):
    rows, cols = candidates[0].shape
    return pl.pallas_call(
        functools.partial(choose_kernel, wanted, hops),
        out_shape=[jax.ShapeDtypeStruct((rows * PARTS, cols), BF16)] * wanted,
        in_specs=[pl.BlockSpec(memory_space=pltpu.SMEM)]
        + [pl.BlockSpec(memory_space=pl.ANY)] * len(candidates),
        scratch_shapes=[pltpu.SemaphoreType.DMA((wanted, PARTS))],
        compiler_params=PARAMS,
        cost_estimate=cost(),
    )(place, *candidates)


def gradients_kernel(units, scale, first, scalar_ref, xt_ref, g_ref, *refs):
    messages, refs = refs[:units], refs[units if first else units + 3 :]
    gg_ref, gu_ref, gd_ref, token_ref = refs
    width = gg_ref.shape[1]
    pass_on(scalar_ref, token_ref)
    for u in range(units):

        @pl.when(pl.program_id(0) == u)
        def _():
            both = dot(xt_ref[...], messages[u][:, width:]) * scale
            gg_ref[...] = both[:, :width].astype(BF16)
            gu_ref[...] = both[:, width:].astype(BF16)
            scaled = messages[u][:, :width]
            gd_ref[...] = (dot(scaled, g_ref[...], ROWS_FIRST) * scale).astype(BF16)


def gradients(scalars, begin, count, scale, x_t, g, messages, grads):
    slots, feats = g.shape
    width = messages[0].shape[1] // 3
    hidden = 2 * count * width
    units = len(messages)

    def at(u, c):
        return c[FIXED + begin + u]

    column = pl.BlockSpec((feats, width), lambda u, c: (0, at(u, c)))
    in_specs = [
        pl.BlockSpec((feats, slots), lambda u, c: (0, 0)),
        pl.BlockSpec((slots, feats), lambda u, c: (0, 0)),
    ]
    in_specs += [pl.BlockSpec((slots, 3 * width), lambda u, c: (0, 0))] * units
    operands = [x_t, g, *messages]
    aliases = {}
    if grads is not None:
        aliases = {len(operands) + 1 + n: n for n in range(3)}
        operands += grads
        in_specs += [pl.BlockSpec(memory_space=pl.ANY)] * 3
    *grads, token = pl.pallas_call(
        functools.partial(gradients_kernel, units, scale, grads is None),
        out_shape=[
            jax.ShapeDtypeStruct((feats, hidden), BF16),
            jax.ShapeDtypeStruct((feats, hidden), BF16),
            jax.ShapeDtypeStruct((hidden, feats), BF16),
            jax.ShapeDtypeStruct(scalars.shape, jnp.int32),
        ],
        grid_spec=pltpu.PrefetchScalarGridSpec(
            num_scalar_prefetch=1,
            grid=(units,),
            in_specs=in_specs,
            out_specs=[
                column,
                column,
                pl.BlockSpec((width, feats), lambda u, c: (at(u, c), 0)),
                pl.BlockSpec(memory_space=pltpu.SMEM),
            ],
        ),
        input_output_aliases=aliases,
        compiler_params=PARAMS,
        cost_estimate=cost(),
    )(scalars, *operands)
    return grads, token


def sum_rows_kernel(units, pieces, scalar_ref, *refs):
    messages, weights, refs = refs[:units], refs[units : 3 * units], refs[3 * units :]
    width = weights[0].shape[1]
    both = jnp.concatenate([message[:, width:] for message in messages], axis=1)
    part = dot(both, jnp.concatenate([w[...] for w in weights], axis=1), LAST_DIMS)
    if not pieces:
        out_ref, token_ref = refs
        out_ref[...] = part
        pass_on(scalar_ref, token_ref)
        return
    acc_in, *outs, acc = refs
    acc[...] = acc_in[...] + part
    size = outs[0].shape[0]
    for n, out in enumerate(outs):
        start = pl.multiple_of((scalar_ref[1] ^ n) * size, size)
        out[...] = acc[pl.ds(start, size), :].astype(BF16)


def sum_rows(scalars, begin, messages, weights, acc, pieces):
    slots, width = messages[0].shape[0], messages[0].shape[1] // 3
    feats = weights[0].shape[0]
    units = len(messages)
    in_specs = [pl.BlockSpec((slots, 3 * width), lambda n, c: (0, 0))] * units
    operands = list(messages)
    for u in range(units):
        column = pl.BlockSpec((feats, width), lambda n, c, u=u: (0, c[FIXED + begin + u]))
        operands += in_hbm(*weights)
        in_specs += [column, column]
    whole = pl.BlockSpec((slots, feats), lambda n, c: (0, 0))
    if pieces:
        operands.append(acc)
        in_specs.append(whole)
        out_shape = [jax.ShapeDtypeStruct((slots // pieces, feats), BF16)] * pieces
        out_specs = [pl.BlockSpec((slots // pieces, feats), lambda n, c: (0, 0))] * pieces
        scratch = [pltpu.VMEM((slots, feats), F32)]
    else:
        out_shape = [
            jax.ShapeDtypeStruct((slots, feats), F32),
            jax.ShapeDtypeStruct(scalars.shape, jnp.int32),
        ]
        out_specs = [whole, pl.BlockSpec(memory_space=pltpu.SMEM)]
        scratch = []
    return pl.pallas_call(
        functools.partial(sum_rows_kernel, units, pieces),
        out_shape=out_shape,
        grid_spec=pltpu.PrefetchScalarGridSpec(
            num_scalar_prefetch=1,
            grid=(1,),
            in_specs=in_specs,
            out_specs=out_specs,
            scratch_shapes=scratch,
        ),
        compiler_params=PARAMS,
        cost_estimate=cost(),
    )(scalars, *operands)


def body(tokens, grad_out, expert_ids, route_weights, w_gate, w_up, w_down):
    experts = lax.axis_size("expert")
    groups = lax.axis_size("dp")
    tok_rows = tokens.shape[0]
    feats = w_gate.shape[1]
    capacity = tok_rows // 2
    chips = groups // 2
    count = chips
    assert groups == 2 * experts and tokens.shape[1] == 2 * feats
    inv_root = 1.0 / math.sqrt(tok_rows * groups)
    expert = lax.axis_index("expert").astype(jnp.int32)
    block = lax.axis_index("dp").astype(jnp.int32)
    chip, core = block // 2, block % 2
    along = jnp.where(core == 0, chip, chips - 1 - chip)
    w_gate, w_up, w_down = w_gate[0], w_up[0], w_down[0]
    ids, weights = expert_ids.T, route_weights.T

    swap = [(j, j ^ 1) for j in range(groups)]
    up = [2 * z for z in range(chips)]
    circle = up + [j + 1 for j in reversed(up)]
    ring = list(zip(circle, circle[1:] + circle[:1]))

    scalars = [along, expert + experts * core, block % experts, block // experts, expert]
    scalars += [(d ^ 1 ^ core) * count + k for d in range(2) for k in range(count)]
    scalars += [(1 - core) * count + (i - (chips - 1 - along)) % count for i in range(count)]
    scalars += [core * count + (i - along) % count for i in range(count)]
    scalars = jnp.stack(scalars).astype(jnp.int32)

    def exchange(messages):
        came = [messages[0]]
        for t in range(1, experts):
            came.append(lax.ppermute(messages[t], "expert", [(q, q ^ t) for q in range(experts)]))
        blocks, token = assemble(scalars, came)
        blocks = blocks.reshape(groups, capacity, feats)
        blocks = lax.all_to_all(blocks, "dp", split_axis=0, concat_axis=0, tiled=True)
        return blocks.reshape(groups * capacity, feats), token

    x_messages, hot, token = dispatch_rows(scalars, ids, weights, tokens, experts, False)
    g_messages, _, _ = dispatch_rows(token, ids, weights, grad_out, experts, True)
    x, _ = exchange(x_messages)
    g, token = exchange(g_messages)

    other_gu, x_t, _ = gate_up(token, x, w_gate, w_up, count, None)
    sib_gu = lax.ppermute(other_gu, "dp", swap)
    both_gu, token = gate_up(scalars, x, w_gate, w_up, count, sib_gu)
    spans = ((0, count // 2), (count // 2, count - count // 2))
    others = [
        lax.ppermute(back_rows(token, g, w_down, begin, size, count, None), "dp", swap)
        for begin, size in spans
    ]
    sums = []
    for (begin, size), sib in zip(spans, others):
        both_b = back_rows(scalars, g, w_down, begin, size, count, sib)
        sums += [((both_gu, begin + i), (both_b, i)) for i in range(size)]

    slots = 2 * count + chips - 2
    first_back = chips - 1 + count
    recv = []
    both = (w_gate, w_up)
    place = along.astype(jnp.int32)[None]
    for s in range(slots):
        came = []
        for part in range(PARTS):
            send = recv[s - 1][part] if s else None
            if s < first_back:
                send = hop(place, s, count, chips, send, sums[s % count], part)
            came.append(lax.ppermute(send, "dp", ring))
        recv.append(came)

    def pick(begin, wanted):
        found = recv[count - 1 + begin : count - 1 + begin + chips + wanted - 1]
        return choose(place, wanted, chips, [part for came in found for part in came])

    early = count - 1
    mine = pick(0, early)
    others = [lax.ppermute(message, "dp", swap) for message in mine]
    grads, token = gradients(scalars, 0, count, inv_root, x_t, g, mine, None)
    acc, token = sum_rows(token, 0, mine, both, None, 0)
    mine = pick(early, count - early)
    others += [lax.ppermute(message, "dp", swap) for message in mine]
    units = [*mine, *others]
    pieces = sum_rows(scalars, early, units, both, acc, groups)
    returned = []
    for r, piece in enumerate(pieces):
        pairs = []
        for q in range(experts):
            for b in range(groups):
                h, e = divmod(b ^ r, experts)
                pairs.append((e * groups + 2 * q + h, q * groups + b))
        returned.append(lax.ppermute(piece, ("expert", "dp"), pairs))
    grads, _ = gradients(scalars, early, count, inv_root, x_t, g, units, grads)
    grad_tokens = combine_rows(scalars, hot, returned, experts)
    return (grad_tokens, grads[0][None], grads[1][None], grads[2][None])


def solution(mesh):
    in_specs = (
        P("dp", "expert"),
        P("dp", "expert"),
        P("dp", None),
        P("dp", None),
        P("expert", "dp", None),
        P("expert", "dp", None),
        P("expert", None, "dp"),
    )
    out_specs = (
        P("dp", "expert"),
        P("expert", "dp", None),
        P("expert", "dp", None),
        P("expert", None, "dp"),
    )
    return jax.shard_map(body, mesh=mesh, in_specs=in_specs, out_specs=out_specs, check_vma=False)
```

profile of v0, /device:TPU:0, one launch (start us, length us, event | category | flops | bytes accessed | tf_op | source)
XLA Modules:
  0.0 226.3 jit_solution(17926337735725637313)
XLA Ops:
  3.4 3.0 %collective-permute-start = (bf16[2,64,896]{2,1,0:T(8,128)(2,1)S(1)}, bf16[2,64,896]{2,1,0:T(8,128)(2,1)S(1)}, u32[]{:S(2)}, u32[]{:S(2)}) collective-permute-start(bf16[2,64,896]{2,1,0:T(8,128)(2,1)S(1)} %get-tuple-element.42), channel_id=1, source_target_pairs={{0,8},{8,0},{16,24},{24,16},{1,9},{9,1},{17,25},{25,17},{2,10},{10... | collective-permute-start | bytes 688136 | tf_op jit(solution)/shard_map/ppermute | solution.py:552
  7.9 4.9 %collective-permute-done.refs_1_ = bf16[2,64,896]{2,1,0:T(8,128)(2,1)S(1)} collective-permute-done((bf16[2,64,896]{2,1,0:T(8,128)(2,1)S(1)}, bf16[2,64,896]{2,1,0:T(8,128)(2,1)S(1)}, u32[]{:S(2)}, u32[]{:S(2)}) %collective-permute-start) | collective-permute-done | bytes 229408 | tf_op jit(solution)/shard_map/ppermute | solution.py:552
  12.8 5.5 %collective-permute-done.1.refs_2_ = bf16[2,64,896]{2,1,0:T(8,128)(2,1)S(1)} collective-permute-done((bf16[2,64,896]{2,1,0:T(8,128)(2,1)S(1)}, bf16[2,64,896]{2,1,0:T(8,128)(2,1)S(1)}, u32[]{:S(2)}, u32[]{:S(2)}) %collective-permute-start.1) | collective-permute-done | bytes 229408 | tf_op jit(solution)/shard_map/ppermute | solution.py:552
  18.4 2.7 %shard_map.103 = (bf16[4,2,64,896]{3,2,1,0:T(8,128)(2,1)}, s32[21]{0:T(128)}) custom-call(s32[21]{0:T(128)S(1)} %stack.87.scalar_ref, bf16[2,64,896]{2,1,0:T(8,128)(2,1)S(1)} %get-tuple-element.41.refs_0_, bf16[2,64,896]{2,1,0:T(8,128)(2,1)S(1)} %collective-permute-done.refs_1_, bf16[2,64,896]{2,1,0:T(8,128)(2,1)S(1)} %collective-permute-done.1.refs_2_, ...), custom_call_target="tpu_custom_call" | custom-call | flops 1024 | bytes 1024 | tf_op jit(solution)/shard_map/pallas_call | solution.py:132
  21.1 4.9 %all-to-all-start = ((bf16[8,64,896]{2,1,0:T(8,128)(2,1)}), bf16[8,64,896]{2,1,0:T(8,128)(2,1)S(1)}, u32[]{:S(2)}, u32[]{:S(2)}) async-start(bf16[8,64,896]{2,1,0:T(8,128)(2,1)} %bitcast.23), calls=%async_computation | async-start | bytes 1835008 | tf_op jit(solution)/shard_map/all_to_all | solution.py:555
  32.1 4.9 %collective-permute-done.3.refs_1_ = bf16[2,64,896]{2,1,0:T(8,128)(2,1)S(1)} collective-permute-done((bf16[2,64,896]{2,1,0:T(8,128)(2,1)S(1)}, bf16[2,64,896]{2,1,0:T(8,128)(2,1)S(1)}, u32[]{:S(2)}, u32[]{:S(2)}) %collective-permute-start.3) | collective-permute-done | bytes 229408 | tf_op jit(solution)/shard_map/ppermute | solution.py:552
  37.0 3.9 %collective-permute-done.4.refs_2_ = bf16[2,64,896]{2,1,0:T(8,128)(2,1)S(1)} collective-permute-done((bf16[2,64,896]{2,1,0:T(8,128)(2,1)S(1)}, bf16[2,64,896]{2,1,0:T(8,128)(2,1)S(1)}, u32[]{:S(2)}, u32[]{:S(2)}) %collective-permute-start.4) | collective-permute-done | bytes 229408 | tf_op jit(solution)/shard_map/ppermute | solution.py:552
  45.8 4.0 %all-to-all-done = bf16[8,64,896]{2,1,0:T(8,128)(2,1)S(1)} async-done(((bf16[8,64,896]{2,1,0:T(8,128)(2,1)}), bf16[8,64,896]{2,1,0:T(8,128)(2,1)S(1)}, u32[]{:S(2)}, u32[]{:S(2)}) %all-to-all-start) | async-done | bytes 917536 | tf_op jit(solution)/shard_map/all_to_all | solution.py:555
  49.8 6.6 %shard_map.106 = (bf16[4,512,512]{2,1,0:T(8,128)(2,1)}, bf16[896,512]{1,0:T(8,128)(2,1)S(1)}, s32[21]{0:T(128)}) custom-call(s32[21]{0:T(128)S(1)} %get-tuple-element.51.scalar_ref, bf16[512,896]{1,0:T(8,128)(2,1)S(1)} %bitcast.39, bf16[896,2048]{1,0:T(8,128)(2,1)} %bitcast.42, bf16[896,2048]{1,0:T(8,128)(2,1)} %bitcast.52), custom_call_target="tpu_custom_call" | custom-call | flops 1024 | bytes 1024 | tf_op jit(solution)/shard_map/pallas_call | solution.py:247
  57.4 3.6 %all-to-all-start.1 = ((bf16[8,64,896]{2,1,0:T(8,128)(2,1)}), bf16[8,64,896]{2,1,0:T(8,128)(2,1)S(1)}, u32[]{:S(2)}, u32[]{:S(2)}) async-start(bf16[8,64,896]{2,1,0:T(8,128)(2,1)} %bitcast.41), calls=%async_computation.1 | async-start | bytes 1835008 | tf_op jit(solution)/shard_map/all_to_all | solution.py:555
  65.9 5.4 %shard_map.107 = (bf16[4,512,512]{2,1,0:T(8,128)(2,1)S(1)}, s32[21]{0:T(128)S(1)}) custom-call(s32[21]{0:T(128)S(1)} %stack.87.scalar_ref, bf16[512,896]{1,0:T(8,128)(2,1)S(1)} %bitcast.40, bf16[896,2048]{1,0:T(8,128)(2,1)} %bitcast.43, bf16[896,2048]{1,0:T(8,128)(2,1)} %bitcast.53, bf16[4,512,512]{2,1,0:T(8,128)(2,1)S(1)} %copy-done.5), custom_call_target="tpu_custom_call" | custom-call | flops 1024 | bytes 1024 | tf_op jit(solution)/shard_map/pallas_call | solution.py:247
  71.2 13.4 %all-to-all-done.1 = bf16[8,64,896]{2,1,0:T(8,128)(2,1)S(1)} async-done(((bf16[8,64,896]{2,1,0:T(8,128)(2,1)}), bf16[8,64,896]{2,1,0:T(8,128)(2,1)S(1)}, u32[]{:S(2)}, u32[]{:S(2)}) %all-to-all-start.1) | async-done | bytes 917536 | tf_op jit(solution)/shard_map/all_to_all | solution.py:555
  103.9 2.6 %shard_map.113.refs_2_ = bf16[2,512,256]{2,1,0:T(8,128)(2,1)S(1)} custom-call(s32[21]{0:T(128)S(1)} %stack.87.scalar_ref, bf16[512,896]{1,0:T(8,128)(2,1)S(1)} %bitcast.36, bf16[2048,896]{1,0:T(8,128)(2,1)} %bitcast.65, bf16[2,512,256]{2,1,0:T(8,128)(2,1)S(1)} %collective-permute-done.10.refs_0_), custom_call_target="tpu_custom_call" | custom-call | flops 1024 | bytes 1024 | tf_op jit(solution)/shard_map/pallas_call | solution.py:277
  122.4 2.6 %collective-permute-start.13 = (bf16[256,768]{1,0:T(8,128)(2,1)S(1)}, bf16[256,768]{1,0:T(8,128)(2,1)S(1)}, u32[]{:S(2)}, u32[]{:S(2)}) collective-permute-start(bf16[256,768]{1,0:T(8,128)(2,1)S(1)} %shard_map.116), channel_id=1, source_target_pairs={{0,2},{2,4},{4,6},{6,7},{7,5},{5,3},{3,1},{1,0},{8,10},{10,12},{12... | collective-permute-start | bytes 1179656 | tf_op jit(solution)/shard_map/ppermute | solution.py:587
  126.6 2.6 %collective-permute-start.20 = (bf16[256,768]{1,0:T(8,128)(2,1)S(1)}, bf16[256,768]{1,0:T(8,128)(2,1)S(1)}, u32[]{:S(2)}, u32[]{:S(2)}) collective-permute-start(bf16[256,768]{1,0:T(8,128)(2,1)S(1)} %shard_map.123), channel_id=1, source_target_pairs={{0,2},{2,4},{4,6},{6,7},{7,5},{5,3},{3,1},{1,0},{8,10},{10,12},{12... | collective-permute-start | bytes 1179656 | tf_op jit(solution)/shard_map/ppermute | solution.py:587
  173.1 4.1 %collective-permute-done.28.refs_7_ = bf16[256,768]{1,0:T(8,128)(2,1)S(1)} collective-permute-done((bf16[256,768]{1,0:T(8,128)(2,1)S(1)}, bf16[256,768]{1,0:T(8,128)(2,1)S(1)}, u32[]{:S(2)}, u32[]{:S(2)}) %collective-permute-start.28) | collective-permute-done | bytes 393248 | tf_op jit(solution)/shard_map/ppermute | solution.py:587
  179.2 4.6 %shard_map.128 = (bf16[896,2048]{1,0:T(8,128)(2,1)}, bf16[896,2048]{1,0:T(8,128)(2,1)}, bf16[2048,896]{1,0:T(8,128)(2,1)}, s32[21]{0:T(128)S(1)}) custom-call(s32[21]{0:T(128)S(1)} %stack.87.scalar_ref, bf16[896,512]{1,0:T(8,128)(2,1)S(1)} %copy-done.3, bf16[512,896]{1,0:T(8,128)(2,1)S(1)} %bitcast.37, bf16[512,768]{1,0:T(8,128)(2,1)S(1)} %get-tuple-element.56.refs_0_, ...), custom_call_target="tpu_custom_call" | custom-call | flops 1024 | bytes 1024 | tf_op jit(solution)/shard_map/pallas_call | solution.py:438
  183.8 4.1 %shard_map.129 = (f32[512,896]{1,0:T(8,128)S(1)}, s32[21]{0:T(128)}) custom-call(s32[21]{0:T(128)S(1)} %get-tuple-element.60.scalar_ref, bf16[512,768]{1,0:T(8,128)(2,1)S(1)} %get-tuple-element.56.refs_0_, bf16[512,768]{1,0:T(8,128)(2,1)S(1)} %get-tuple-element.57.refs_1_, bf16[512,768]{1,0:T(8,128)(2,1)S(1)} %get-tuple-element.58.refs_2_, ...), custom_call_target="tpu_custom_call" | custom-call | flops 1024 | bytes 1024 | tf_op jit(solution)/shard_map/pallas_call | solution.py:506
  188.0 5.9 %shard_map.130 = (bf16[64,896]{1,0:T(8,128)(2,1)S(1)}, bf16[64,896]{1,0:T(8,128)(2,1)S(1)}, bf16[64,896]{1,0:T(8,128)(2,1)S(1)}, bf16[64,896]{1,0:T(8,128)(2,1)S...) custom-call(s32[21]{0:T(128)S(1)} %stack.87.scalar_ref, ...), custom_call_target="tpu_custom_call" | custom-call | flops 1024 | bytes 1024 | tf_op jit(solution)/shard_map/pallas_call | solution.py:506
  196.8 2.6 %collective-permute-start.35 = (bf16[64,896]{1,0:T(8,128)(2,1)S(1)}, bf16[64,896]{1,0:T(8,128)(2,1)S(1)}, u32[]{:S(2)}, u32[]{:S(2)}) collective-permute-start(bf16[64,896]{1,0:T(8,128)(2,1)S(1)} %get-tuple-element.64), channel_id=1, source_target_pairs={{16,0},{24,1},{0,2},{8,3},{17,4},{25,5},{1,6},{9,7},{18,8},{26,9},... | collective-permute-start | bytes 344072 | tf_op jit(solution)/shard_map/ppermute | solution.py:610
  199.4 5.5 %collective-permute-start.36 = (bf16[64,896]{1,0:T(8,128)(2,1)S(1)}, bf16[64,896]{1,0:T(8,128)(2,1)S(1)}, u32[]{:S(2)}, u32[]{:S(2)}) collective-permute-start(bf16[64,896]{1,0:T(8,128)(2,1)S(1)} %get-tuple-element.65), channel_id=1, source_target_pairs={{24,0},{16,1},{8,2},{0,3},{25,4},{17,5},{9,6},{1,7},{26,8},{18,9},... | collective-permute-start | bytes 344072 | tf_op jit(solution)/shard_map/ppermute | solution.py:610
  206.3 5.0 %collective-permute-start.38 = (bf16[64,896]{1,0:T(8,128)(2,1)S(1)}, bf16[64,896]{1,0:T(8,128)(2,1)S(1)}, u32[]{:S(2)}, u32[]{:S(2)}) collective-permute-start(bf16[64,896]{1,0:T(8,128)(2,1)S(1)} %get-tuple-element.67), channel_id=1, source_target_pairs={{9,0},{1,1},{25,2},{17,3},{8,4},{0,5},{24,6},{16,7},{11,8},{3,9},{... | collective-permute-start | bytes 344072 | tf_op jit(solution)/shard_map/ppermute | solution.py:610
  215.7 6.6 %shard_map.132 = (bf16[896,2048]{1,0:T(8,128)(2,1)}, bf16[896,2048]{1,0:T(8,128)(2,1)}, bf16[2048,896]{1,0:T(8,128)(2,1)}, s32[21]{0:T(128)}) custom-call(s32[21]{0:T(128)S(1)} %stack.87.scalar_ref, bf16[896,512]{1,0:T(8,128)(2,1)S(1)} %copy-done.3, bf16[512,896]{1,0:T(8,128)(2,1)S(1)} %bitcast.38, ...), custom_call_target="tpu_custom_call", output_to_operand_aliasing={{0}: (8, {}), {1}: (9, {}), {2}: (10, {})} | custom-call | flops 1024 | bytes 1024 | tf_op jit(solution)/shard_map/pallas_call | solution.py:438
  223.2 2.9 %shard_map.131 = bf16[128,1792]{1,0:T(8,128)(2,1)} custom-call(s32[21]{0:T(128)S(1)} %stack.87.scalar_ref, bf16[256,128]{1,0:T(8,128)(2,1)S(1)} %get-tuple-element.40.hot_ref, bf16[64,896]{1,0:T(8,128)(2,1)} %copy-done.7, bf16[64,896]{1,0:T(8,128)(2,1)} %copy-done.8, bf16[64,896]{1,0:T(8,128)(2,1)} %copy-done.9, bf16[64,896]{1,0:T(8,128)(2,1)} %copy-done.10, ...), custom_call_target="tpu_custom_call" | custom-call | flops 1024 | bytes 1024 | tf_op jit(solution)/shard_map/pallas_call | solution.py:189
  (124 shorter events, 113.0 us)
Async XLA Ops:
  3.4 9.4 %collective-permute-start = (bf16[2,64,896]{2,1,0:T(8,128)(2,1)S(1)}, bf16[2,64,896]{2,1,0:T(8,128)(2,1)S(1)}, u32[]{:S(2)}, u32[]{:S(2)}) collective-permute-start(bf16[2,64,896]{2,1,0:T(8,128)(2,1)S(1)} %get-tuple-element.42), channel_id=1, source_target_pairs={{0,8},{8,0},{16,24},{24,16},{1,9},{9,1},{17,25},{25,17},{2,10},{10... | collective-permute-start | bytes 688136 | tf_op jit(solution)/shard_map/ppermute | solution.py:552
  6.4 12.0 %collective-permute-start.1 = (bf16[2,64,896]{2,1,0:T(8,128)(2,1)S(1)}, bf16[2,64,896]{2,1,0:T(8,128)(2,1)S(1)}, u32[]{:S(2)}, u32[]{:S(2)}) collective-permute-start(bf16[2,64,896]{2,1,0:T(8,128)(2,1)S(1)} %get-tuple-element.43), channel_id=1, source_target_pairs={{0,16},{8,24},{16,0},{24,8},{1,17},{9,25},{17,1},{25,9},{2,18},{10... | collective-permute-start | bytes 688136 | tf_op jit(solution)/shard_map/ppermute | solution.py:552
  7.9 10.5 %collective-permute-start.2 = (bf16[2,64,896]{2,1,0:T(8,128)(2,1)S(1)}, bf16[2,64,896]{2,1,0:T(8,128)(2,1)S(1)}, u32[]{:S(2)}, u32[]{:S(2)}) collective-permute-start(bf16[2,64,896]{2,1,0:T(8,128)(2,1)S(1)} %get-tuple-element.44), channel_id=1, source_target_pairs={{0,24},{8,16},{16,8},{24,0},{1,25},{9,17},{17,9},{25,1},{2,26},{10... | collective-permute-start | bytes 688136 | tf_op jit(solution)/shard_map/ppermute | solution.py:552
  21.1 28.7 %all-to-all-start = ((bf16[8,64,896]{2,1,0:T(8,128)(2,1)}), bf16[8,64,896]{2,1,0:T(8,128)(2,1)S(1)}, u32[]{:S(2)}, u32[]{:S(2)}) async-start(bf16[8,64,896]{2,1,0:T(8,128)(2,1)} %bitcast.23), calls=%async_computation | async-start | bytes 1835008 | tf_op jit(solution)/shard_map/all_to_all | solution.py:555
  28.5 8.5 %collective-permute-start.3 = (bf16[2,64,896]{2,1,0:T(8,128)(2,1)S(1)}, bf16[2,64,896]{2,1,0:T(8,128)(2,1)S(1)}, u32[]{:S(2)}, u32[]{:S(2)}) collective-permute-start(bf16[2,64,896]{2,1,0:T(8,128)(2,1)S(1)} %get-tuple-element.48), channel_id=1, source_target_pairs={{0,8},{8,0},{16,24},{24,16},{1,9},{9,1},{17,25},{25,17},{2,10},{10... | collective-permute-start | bytes 688136 | tf_op jit(solution)/shard_map/ppermute | solution.py:552
  29.8 11.0 %collective-permute-start.4 = (bf16[2,64,896]{2,1,0:T(8,128)(2,1)S(1)}, bf16[2,64,896]{2,1,0:T(8,128)(2,1)S(1)}, u32[]{:S(2)}, u32[]{:S(2)}) collective-permute-start(bf16[2,64,896]{2,1,0:T(8,128)(2,1)S(1)} %get-tuple-element.49), channel_id=1, source_target_pairs={{0,16},{8,24},{16,0},{24,8},{1,17},{9,25},{17,1},{25,9},{2,18},{10... | collective-permute-start | bytes 688136 | tf_op jit(solution)/shard_map/ppermute | solution.py:552
  30.6 11.8 %collective-permute-start.5 = (bf16[2,64,896]{2,1,0:T(8,128)(2,1)S(1)}, bf16[2,64,896]{2,1,0:T(8,128)(2,1)S(1)}, u32[]{:S(2)}, u32[]{:S(2)}) collective-permute-start(bf16[2,64,896]{2,1,0:T(8,128)(2,1)S(1)} %get-tuple-element.50), channel_id=1, source_target_pairs={{0,24},{8,16},{16,8},{24,0},{1,25},{9,17},{17,9},{25,1},{2,26},{10... | collective-permute-start | bytes 688136 | tf_op jit(solution)/shard_map/ppermute | solution.py:552
  57.4 27.3 %all-to-all-start.1 = ((bf16[8,64,896]{2,1,0:T(8,128)(2,1)}), bf16[8,64,896]{2,1,0:T(8,128)(2,1)S(1)}, u32[]{:S(2)}, u32[]{:S(2)}) async-start(bf16[8,64,896]{2,1,0:T(8,128)(2,1)} %bitcast.41), calls=%async_computation.1 | async-start | bytes 1835008 | tf_op jit(solution)/shard_map/all_to_all | solution.py:555
  91.8 9.5 %collective-permute-start.16 = (bf16[256,768]{1,0:T(8,128)(2,1)S(1)}, bf16[256,768]{1,0:T(8,128)(2,1)S(1)}, u32[]{:S(2)}, u32[]{:S(2)}) collective-permute-start(bf16[256,768]{1,0:T(8,128)(2,1)S(1)} %shard_map.119), channel_id=1, source_target_pairs={{0,2},{2,4},{4,6},{6,7},{7,5},{5,3},{3,1},{1,0},{8,10},{10,12},{12... | collective-permute-start | bytes 1179656 | tf_op jit(solution)/shard_map/ppermute | solution.py:587
  94.5 9.4 %collective-permute-start.10 = (bf16[2,512,256]{2,1,0:T(8,128)(2,1)S(1)}, bf16[2,512,256]{2,1,0:T(8,128)(2,1)S(1)}, u32[]{:S(2)}, u32[]{:S(2)}) collective-permute-start(bf16[2,512,256]{2,1,0:T(8,128)(2,1)S(1)} %shard_map.112), channel_id=1, source_target_pairs={{0,1},{1,0},{2,3},{3,2},{4,5},{5,4},{6,7},{7,6},{8,9},{9,8},{10,11... | collective-permute-start | bytes 1572872 | tf_op jit(solution)/shard_map/ppermute | solution.py:568
  97.2 9.3 %collective-permute-start.9 = (bf16[256,768]{1,0:T(8,128)(2,1)S(1)}, bf16[256,768]{1,0:T(8,128)(2,1)S(1)}, u32[]{:S(2)}, u32[]{:S(2)}) collective-permute-start(bf16[256,768]{1,0:T(8,128)(2,1)S(1)} %shard_map.111), channel_id=1, source_target_pairs={{0,2},{2,4},{4,6},{6,7},{7,5},{5,3},{3,1},{1,0},{8,10},{10,12},{12... | collective-permute-start | bytes 1179656 | tf_op jit(solution)/shard_map/ppermute | solution.py:587
  164.5 8.6 %collective-permute-start.27 = (bf16[256,768]{1,0:T(8,128)(2,1)S(1)}, bf16[256,768]{1,0:T(8,128)(2,1)S(1)}, u32[]{:S(2)}, u32[]{:S(2)}) collective-permute-start(bf16[256,768]{1,0:T(8,128)(2,1)S(1)} %collective-permute-done.25.refs_4_.refs_10_), channel_id=1, source_target_pairs={{0,2},{2,4},{4,6},{6,7},{7,5},{5,3},{3,1},{1,0},{8,10},{10,12},{12... | collective-permute-start | bytes 1179656 | tf_op jit(solution)/shard_map/ppermute | solution.py:587
  172.4 15.6 %collective-permute-start.29 = (bf16[512,768]{1,0:T(8,128)(2,1)S(1)}, bf16[512,768]{1,0:T(8,128)(2,1)S(1)}, u32[]{:S(2)}, u32[]{:S(2)}) collective-permute-start(bf16[512,768]{1,0:T(8,128)(2,1)S(1)} %get-tuple-element.56.refs_0_), channel_id=1, source_target_pairs={{0,1},{1,0},{2,3},{3,2},{4,5},{5,4},{6,7},{7,6},{8,9},{9,8},{10,11... | collective-permute-start | bytes 2359304 | tf_op jit(solution)/shard_map/ppermute | solution.py:596
  172.5 15.5 %collective-permute-start.30 = (bf16[512,768]{1,0:T(8,128)(2,1)S(1)}, bf16[512,768]{1,0:T(8,128)(2,1)S(1)}, u32[]{:S(2)}, u32[]{:S(2)}) collective-permute-start(bf16[512,768]{1,0:T(8,128)(2,1)S(1)} %get-tuple-element.57.refs_1_), channel_id=1, source_target_pairs={{0,1},{1,0},{2,3},{3,2},{4,5},{5,4},{6,7},{7,6},{8,9},{9,8},{10,11... | collective-permute-start | bytes 2359304 | tf_op jit(solution)/shard_map/ppermute | solution.py:596
  173.0 15.0 %collective-permute-start.31 = (bf16[512,768]{1,0:T(8,128)(2,1)S(1)}, bf16[512,768]{1,0:T(8,128)(2,1)S(1)}, u32[]{:S(2)}, u32[]{:S(2)}) collective-permute-start(bf16[512,768]{1,0:T(8,128)(2,1)S(1)} %get-tuple-element.58.refs_2_), channel_id=1, source_target_pairs={{0,1},{1,0},{2,3},{3,2},{4,5},{5,4},{6,7},{7,6},{8,9},{9,8},{10,11... | collective-permute-start | bytes 2359304 | tf_op jit(solution)/shard_map/ppermute | solution.py:596
  177.7 10.3 %collective-permute-start.32 = (bf16[512,768]{1,0:T(8,128)(2,1)S(1)}, bf16[512,768]{1,0:T(8,128)(2,1)S(1)}, u32[]{:S(2)}, u32[]{:S(2)}) collective-permute-start(bf16[512,768]{1,0:T(8,128)(2,1)S(1)} %shard_map.126.refs_0_), channel_id=1, source_target_pairs={{0,1},{1,0},{2,3},{3,2},{4,5},{5,4},{6,7},{7,6},{8,9},{9,8},{10,11... | collective-permute-start | bytes 2359304 | tf_op jit(solution)/shard_map/ppermute | solution.py:600
  193.9 12.4 %collective-permute-start.33 = (bf16[64,896]{1,0:T(8,128)(2,1)S(1)}, bf16[64,896]{1,0:T(8,128)(2,1)S(1)}, u32[]{:S(2)}, u32[]{:S(2)}) collective-permute-start(bf16[64,896]{1,0:T(8,128)(2,1)S(1)} %get-tuple-element.62), channel_id=1, source_target_pairs={{0,0},{8,1},{16,2},{24,3},{1,4},{9,5},{17,6},{25,7},{2,8},{10,9},{... | collective-permute-start | bytes 344072 | tf_op jit(solution)/shard_map/ppermute | solution.py:610
  194.6 16.7 %collective-permute-start.34 = (bf16[64,896]{1,0:T(8,128)(2,1)S(1)}, bf16[64,896]{1,0:T(8,128)(2,1)S(1)}, u32[]{:S(2)}, u32[]{:S(2)}) collective-permute-start(bf16[64,896]{1,0:T(8,128)(2,1)S(1)} %get-tuple-element.63), channel_id=1, source_target_pairs={{8,0},{0,1},{24,2},{16,3},{9,4},{1,5},{25,6},{17,7},{10,8},{2,9},{... | collective-permute-start | bytes 344072 | tf_op jit(solution)/shard_map/ppermute | solution.py:610
  196.8 16.5 %collective-permute-start.35 = (bf16[64,896]{1,0:T(8,128)(2,1)S(1)}, bf16[64,896]{1,0:T(8,128)(2,1)S(1)}, u32[]{:S(2)}, u32[]{:S(2)}) collective-permute-start(bf16[64,896]{1,0:T(8,128)(2,1)S(1)} %get-tuple-element.64), channel_id=1, source_target_pairs={{16,0},{24,1},{0,2},{8,3},{17,4},{25,5},{1,6},{9,7},{18,8},{26,9},... | collective-permute-start | bytes 344072 | tf_op jit(solution)/shard_map/ppermute | solution.py:610
  199.4 22.9 %collective-permute-start.36 = (bf16[64,896]{1,0:T(8,128)(2,1)S(1)}, bf16[64,896]{1,0:T(8,128)(2,1)S(1)}, u32[]{:S(2)}, u32[]{:S(2)}) collective-permute-start(bf16[64,896]{1,0:T(8,128)(2,1)S(1)} %get-tuple-element.65), channel_id=1, source_target_pairs={{24,0},{16,1},{8,2},{0,3},{25,4},{17,5},{9,6},{1,7},{26,8},{18,9},... | collective-permute-start | bytes 344072 | tf_op jit(solution)/shard_map/ppermute | solution.py:610
  204.9 17.5 %collective-permute-start.37 = (bf16[64,896]{1,0:T(8,128)(2,1)S(1)}, bf16[64,896]{1,0:T(8,128)(2,1)S(1)}, u32[]{:S(2)}, u32[]{:S(2)}) collective-permute-start(bf16[64,896]{1,0:T(8,128)(2,1)S(1)} %get-tuple-element.66), channel_id=1, source_target_pairs={{1,0},{9,1},{17,2},{25,3},{0,4},{8,5},{16,6},{24,7},{3,8},{11,9},{... | collective-permute-start | bytes 344072 | tf_op jit(solution)/shard_map/ppermute | solution.py:610
  206.3 16.1 %collective-permute-start.38 = (bf16[64,896]{1,0:T(8,128)(2,1)S(1)}, bf16[64,896]{1,0:T(8,128)(2,1)S(1)}, u32[]{:S(2)}, u32[]{:S(2)}) collective-permute-start(bf16[64,896]{1,0:T(8,128)(2,1)S(1)} %get-tuple-element.67), channel_id=1, source_target_pairs={{9,0},{1,1},{25,2},{17,3},{8,4},{0,5},{24,6},{16,7},{11,8},{3,9},{... | collective-permute-start | bytes 344072 | tf_op jit(solution)/shard_map/ppermute | solution.py:610
  211.4 11.1 %collective-permute-start.39 = (bf16[64,896]{1,0:T(8,128)(2,1)S(1)}, bf16[64,896]{1,0:T(8,128)(2,1)S(1)}, u32[]{:S(2)}, u32[]{:S(2)}) collective-permute-start(bf16[64,896]{1,0:T(8,128)(2,1)S(1)} %get-tuple-element.68), channel_id=1, source_target_pairs={{17,0},{25,1},{1,2},{9,3},{16,4},{24,5},{0,6},{8,7},{19,8},{27,9},... | collective-permute-start | bytes 344072 | tf_op jit(solution)/shard_map/ppermute | solution.py:610
  213.3 9.1 %collective-permute-start.40 = (bf16[64,896]{1,0:T(8,128)(2,1)S(1)}, bf16[64,896]{1,0:T(8,128)(2,1)S(1)}, u32[]{:S(2)}, u32[]{:S(2)}) collective-permute-start(bf16[64,896]{1,0:T(8,128)(2,1)S(1)} %get-tuple-element.69), channel_id=1, source_target_pairs={{25,0},{17,1},{9,2},{1,3},{24,4},{16,5},{8,6},{0,7},{27,8},{19,9},... | collective-permute-start | bytes 344072 | tf_op jit(solution)/shard_map/ppermute | solution.py:610
  (34 other events, 232.5 us)
where the time goes:
time: 227 us; the launch traced here: 226 us
  starting transfers between devices  85.2 us (38%)
  waiting for transfers between devices  73.7 us (32%)
  Pallas kernels  59.1 us (26%)
  local copies, waits for them, and re-layouts  6.88 us (3%)
    ppermute x20, starting transfers between devices, body(): came.append(lax.ppermute(send, 'dp', ring))  44.2 us
    ppermute x20, waiting for transfers between devices, body(): came.append(lax.ppermute(send, 'dp', ring))  32.7 us
    ppermute x8, starting transfers between devices, body(): returned.append(lax.ppermute(piece, ('expert', 'dp'), pairs))  21.7 us
    ppermute x6, waiting for transfers between devices, exchange(): lax.ppermute(messages[t], 'expert', [(q, q ^ t) for q in range(experts)])  20.8 us
    all_to_all x2, waiting for transfers between devices, exchange(): lax.all_to_all(blocks, 'dp', split_axis=0, concat_axis=0, tiled=True)  17.4 us
    pallas_call x2, Pallas kernels, gate_up(): pl.pallas_call(functools.partial(gate_up_kernel, own), out_shape=out_shap...  12 us
    pallas_call x2, Pallas kernels, gradients(): pl.pallas_call(functools.partial(gradients_kernel, units, scale, grads is...  11.2 us
    pallas_call x4, Pallas kernels, back_rows(): pl.pallas_call(functools.partial(back_kernel, own), out_shape=jax.ShapeDt...  10.1 us
  transfers between devices with their start and end apart: 43, of which 27 were waited for; matrix products, arithmetic and copies ran while one was open for 0% of the time, Pallas kernels for 15%

commit v1 on v0

--- a/solution.py
+++ b/solution.py
@@ -116,8 +116,7 @@
 
 
 def assemble_kernel(scalar_ref, *refs):
-    *messages, out_ref, token_ref, sems = refs
-    pass_on(scalar_ref, token_ref)
+    *messages, out_ref, sems = refs
 
     def copy(t, message):
         return pltpu.make_async_copy(message, out_ref.at[t ^ scalar_ref[4]], sems.at[t])
@@ -131,13 +130,9 @@
 def assemble(scalars, messages):
     return pl.pallas_call(
         assemble_kernel,
-        out_shape=(
-            jax.ShapeDtypeStruct((len(messages), *messages[0].shape), BF16),
-            jax.ShapeDtypeStruct(scalars.shape, jnp.int32),
-        ),
+        out_shape=jax.ShapeDtypeStruct((len(messages), *messages[0].shape), BF16),
         in_specs=[pl.BlockSpec(memory_space=pltpu.SMEM)]
         + [pl.BlockSpec(memory_space=pl.ANY)] * len(messages),
-        out_specs=(pl.BlockSpec(memory_space=pltpu.VMEM), pl.BlockSpec(memory_space=pltpu.SMEM)),
         scratch_shapes=[pltpu.SemaphoreType.DMA((len(messages),))],
         compiler_params=PARAMS,
         cost_estimate=cost(),
@@ -208,85 +203,84 @@
     return out
 
 
-def gate_up_kernel(own, scalar_ref, x_ref, wg_ref, wu_ref, *refs):
+def gate_up_kernel(scalar_ref, x_ref, wg_ref, wu_ref, *outs):
     width = wg_ref.shape[1]
-    gate = dot(x_ref[...], wg_ref[...])
-    upper = dot(x_ref[...], wu_ref[...])
-    *refs, token_ref = refs
-    pass_on(scalar_ref, token_ref)
-    if own:
-        sib_ref, out_ref = refs
-        gate += sib_ref[0, :, :width].astype(F32)
-        upper += sib_ref[0, :, width:].astype(F32)
-    else:
-        out_ref, turned_ref = refs
-
-        @pl.when(pl.program_id(0) == 0)
+
+    @pl.when((pl.program_id(0) == 0) & (pl.program_id(1) == 0))
+    def _():
+        outs[2][...] = x_ref[...].T
+
+    for own in range(2):
+
+        @pl.when(pl.program_id(1) == own)
         def _():
-            turned_ref[...] = x_ref[...].T
-
-    out_ref[0, :, :width] = gate.astype(BF16)
-    out_ref[0, :, width:] = upper.astype(BF16)
-
-
-def gate_up(scalars, x, w_gate, w_up, count, sib):
+            outs[own][0, :, :width] = dot(x_ref[...], wg_ref[...]).astype(BF16)
+            outs[own][0, :, width:] = dot(x_ref[...], wu_ref[...]).astype(BF16)
+
+
+def gate_up(scalars, x, w_gate, w_up, count):
     slots, feats = x.shape
     width = w_gate.shape[1] // (2 * count)
-    own = sib is not None
-    chunk_spec = pl.BlockSpec((1, slots, 2 * width), lambda i, c: (i, 0, 0))
+    out = jax.ShapeDtypeStruct((count, slots, 2 * width), BF16)
+    out_spec = pl.BlockSpec((1, slots, 2 * width), lambda i, own, c: (i, 0, 0))
     column = pl.BlockSpec(
-        (feats, width), lambda i, c: (0, c[FIXED + 2 * count + own * count + i])
+        (feats, width), lambda i, own, c: (0, c[FIXED + 2 * count + own * count + i])
     )
-    out_shape = [jax.ShapeDtypeStruct((count, slots, 2 * width), BF16)]
-    out_specs = [chunk_spec]
-    if not own:
-        out_shape.append(jax.ShapeDtypeStruct((feats, slots), BF16))
-        out_specs.append(pl.BlockSpec((feats, slots), lambda i, c: (0, 0)))
-    out_shape.append(jax.ShapeDtypeStruct(scalars.shape, jnp.int32))
-    out_specs.append(pl.BlockSpec(memory_space=pltpu.SMEM))
     return pl.pallas_call(
-        functools.partial(gate_up_kernel, own),
-        out_shape=out_shape,
+        gate_up_kernel,
+        out_shape=(out, out, jax.ShapeDtypeStruct((feats, slots), BF16)),
         grid_spec=pltpu.PrefetchScalarGridSpec(
             num_scalar_prefetch=1,
-            grid=(count,),
-            in_specs=[pl.BlockSpec((slots, feats), lambda i, c: (0, 0)), column, column]
-            + [chunk_spec] * own,
-            out_specs=out_specs,
+            grid=(count, 2),
+            in_specs=[pl.BlockSpec((slots, feats), lambda i, own, c: (0, 0)), column, column],
+            out_specs=(
+                out_spec,
+                out_spec,
+                pl.BlockSpec((feats, slots), lambda i, own, c: (0, 0)),
+            ),
         ),
         compiler_params=PARAMS,
         cost_estimate=cost(),
-    )(scalars, x, *in_hbm(w_gate, w_up), *([sib] if own else []))
-
-
-def back_kernel(own, scalar_ref, g_ref, wd_ref, *refs):
+    )(scalars, x, *in_hbm(w_gate, w_up))
+
+
+def back_kernel(scalar_ref, g_ref, wd_ref, *refs):
+    *shares, out_ref = refs
     back = dot(g_ref[...], wd_ref[...], LAST_DIMS)
-    if own:
-        back += refs[0][0].astype(F32)
-    refs[-1][0] = back.astype(BF16)
-
-
-def back_rows(scalars, g, w_down, begin, size, count, sib):
+    if not shares:
+        out_ref[0] = back.astype(BF16)
+        return
+    sib_b, own_gu, sib_gu = shares
+    width = back.shape[1]
+    both = own_gu[0].astype(F32) + sib_gu[0].astype(F32)
+    out_ref[0, :, : 2 * width] = both.astype(BF16)
+    out_ref[0, :, 2 * width :] = (back + sib_b[0].astype(F32)).astype(BF16)
+
+
+def back_rows(scalars, g, w_down, begin, size, count, shares):
     slots, feats = g.shape
     width = w_down.shape[0] // (2 * count)
-    own = sib is not None
-    chunk_spec = pl.BlockSpec((1, slots, width), lambda i, c: (i, 0, 0))
+    own = bool(shares)
     row = pl.BlockSpec(
         (width, feats), lambda i, c: (c[FIXED + 2 * count + own * count + begin + i], 0)
     )
+    in_specs = [pl.BlockSpec((slots, feats), lambda i, c: (0, 0)), row]
+    if own:
+        in_specs.append(pl.BlockSpec((1, slots, width), lambda i, c: (i, 0, 0)))
+        in_specs += [pl.BlockSpec((1, slots, 2 * width), lambda i, c: (begin + i, 0, 0))] * 2
+    cols = (3 if own else 1) * width
     return pl.pallas_call(
-        functools.partial(back_kernel, own),
-        out_shape=jax.ShapeDtypeStruct((size, slots, width), BF16),
+        back_kernel,
+        out_shape=jax.ShapeDtypeStruct((size, slots, cols), BF16),
         grid_spec=pltpu.PrefetchScalarGridSpec(
             num_scalar_prefetch=1,
             grid=(size,),
-            in_specs=[pl.BlockSpec((slots, feats), lambda i, c: (0, 0)), row]
-            + [chunk_spec] * own,
-            out_specs=chunk_spec,
+            in_specs=in_specs,
+            out_specs=pl.BlockSpec((1, slots, cols), lambda i, c: (i, 0, 0)),
         ),
         compiler_params=PARAMS,
         cost_estimate=cost(),
-    )(scalars, g, *in_hbm(w_down), *([sib] if own else []))
+    )(scalars, g, *in_hbm(w_down), *shares)
 
 
 def activate(gate, upper, back):
@@ -301,7 +295,7 @@
 
 def hop_kernel(plan, scalar_ref, *refs):
     slot, count, chips, came = plan
-    gate_up_ref, back_ref = refs[-3:-1]
+    sums_ref = refs[-2]
     recv_ref = refs[0] if came else None
     send_ref = refs[-1]
     at = scalar_ref[0]
@@ -310,7 +304,7 @@
 
     def total(part):
         columns = slice(part * width, (part + 1) * width)
-        value = (gate_up_ref[0, :, columns] if part < 2 else back_ref[0]).astype(F32)
+        value = sums_ref[0, :, columns].astype(F32)
         if came:
             value += jnp.where(at > 0, recv_ref[:, columns].astype(F32), 0.0)
         return value
@@ -333,18 +327,15 @@
 
 
 def hop(scalars, slot, count, chips, recv, sums, part):
-    rows = sums[0][0].shape[1] // PARTS
-    cols = sums[0][0].shape[2] + sums[1][0].shape[2]
+    array, i = sums
+    rows, cols = array.shape[1] // PARTS, array.shape[2]
     message = pl.BlockSpec((rows, cols), lambda n, c: (0, 0))
     operands, in_specs = [], []
     if recv is not None:
         operands.append(recv)
         in_specs.append(message)
-    for array, i in sums:
-        operands.append(array)
-        in_specs.append(
-            pl.BlockSpec((1, rows, array.shape[2]), lambda n, c, i=i: (i, part, 0))
-        )
+    operands.append(array)
+    in_specs.append(pl.BlockSpec((1, rows, cols), lambda n, c: (i, part, 0)))
     plan = (slot, count, chips, recv is not None)
     return pl.pallas_call(
         functools.partial(hop_kernel, plan),
@@ -550,33 +541,32 @@
         came = [messages[0]]
         for t in range(1, experts):
             came.append(lax.ppermute(messages[t], "expert", [(q, q ^ t) for q in range(experts)]))
-        blocks, token = assemble(scalars, came)
-        blocks = blocks.reshape(groups, capacity, feats)
+        blocks = assemble(scalars, came).reshape(groups, capacity, feats)
         blocks = lax.all_to_all(blocks, "dp", split_axis=0, concat_axis=0, tiled=True)
-        return blocks.reshape(groups * capacity, feats), token
+        return blocks.reshape(groups * capacity, feats)
 
     x_messages, hot, token = dispatch_rows(scalars, ids, weights, tokens, experts, False)
     g_messages, _, _ = dispatch_rows(token, ids, weights, grad_out, experts, True)
-    x, _ = exchange(x_messages)
-    g, token = exchange(g_messages)
-
-    other_gu, x_t, _ = gate_up(token, x, w_gate, w_up, count, None)
+    x = exchange(x_messages)
+    g = exchange(g_messages)
+
+    other_gu, own_gu, x_t = gate_up(scalars, x, w_gate, w_up, count)
     sib_gu = lax.ppermute(other_gu, "dp", swap)
-    both_gu, token = gate_up(scalars, x, w_gate, w_up, count, sib_gu)
     spans = ((0, count // 2), (count // 2, count - count // 2))
     others = [
-        lax.ppermute(back_rows(token, g, w_down, begin, size, count, None), "dp", swap)
+        lax.ppermute(back_rows(scalars, g, w_down, begin, size, count, ()), "dp", swap)
         for begin, size in spans
     ]
     sums = []
-    for (begin, size), sib in zip(spans, others):
-        both_b = back_rows(scalars, g, w_down, begin, size, count, sib)
-        sums += [((both_gu, begin + i), (both_b, i)) for i in range(size)]
+    for (begin, size), sib_b in zip(spans, others):
+        shares = (sib_b, own_gu, sib_gu)
+        both = back_rows(scalars, g, w_down, begin, size, count, shares)
+        sums += [(both, i) for i in range(size)]
 
     slots = 2 * count + chips - 2
     first_back = chips - 1 + count
     recv = []
-    both = (w_gate, w_up)
+    gate_and_up = (w_gate, w_up)
     place = along.astype(jnp.int32)[None]
     for s in range(slots):
         came = []
@@ -587,19 +577,20 @@
             came.append(lax.ppermute(send, "dp", ring))
         recv.append(came)
 
-    def pick(begin, wanted):
+    def pick(token, begin, wanted):
         found = recv[count - 1 + begin : count - 1 + begin + chips + wanted - 1]
-        return choose(place, wanted, chips, [part for came in found for part in came])
+        return choose(token, wanted, chips, [part for came in found for part in came])
 
     early = count - 1
-    mine = pick(0, early)
+    mine = pick(place, 0, early)
     others = [lax.ppermute(message, "dp", swap) for message in mine]
     grads, token = gradients(scalars, 0, count, inv_root, x_t, g, mine, None)
-    acc, token = sum_rows(token, 0, mine, both, None, 0)
-    mine = pick(early, count - early)
+    last = pick(token, early, count - early)
+    acc, _ = sum_rows(token, 0, mine, gate_and_up, None, 0)
+    mine = last
     others += [lax.ppermute(message, "dp", swap) for message in mine]
     units = [*mine, *others]
-    pieces = sum_rows(scalars, early, units, both, acc, groups)
+    pieces = sum_rows(scalars, early, units, gate_and_up, acc, groups)
     returned = []
     for r, piece in enumerate(pieces):
         pairs = []

time: 227 us -> 216 us (0.952)
  waiting for transfers between devices: 73.7 us -> 66.4 us
  local copies, waits for them, and re-layouts: 6.88 us -> 2.95 us
    ppermute x20, waiting for transfers between devices: 32.7 us -> 28.6 us  [body(): came.append(lax.ppermute(send, 'dp', ring))]
    unnamed x30 -> x24, local copies, waits for them, and re-layouts: 6.78 us -> 2.85 us
    all_to_all x2, waiting for transfers between devices: 17.4 us -> 15.1 us  [exchange(): lax.all_to_all(blocks, 'dp', split_axis=0, concat_axis=0, tiled=True)]
    pallas_call x8 -> x7, Pallas kernels: 27.2 us -> 27.3 us  [the longest x4 11.2 us: back_rows(): pl.pallas_call(back_kernel, out_shape=jax.ShapeDtypeStruct((size, slots,...]
  transfers between devices with their start and end apart: 43 -> 43, of which waited for: 27 -> 25; matrix products, arithmetic and copies ran while one was open for 0% -> 0% of each run, Pallas kernels for 15% -> 20%
where the time goes in v1:
time: 216 us; the launch traced here: 215 us
  starting transfers between devices  84.3 us (39%)
  waiting for transfers between devices  66.4 us (31%)
  Pallas kernels  59.8 us (28%)
  local copies, waits for them, and re-layouts  2.95 us (1%)
    ppermute x20, starting transfers between devices, body(): came.append(lax.ppermute(send, 'dp', ring))  43.7 us
    ppermute x20, waiting for transfers between devices, body(): came.append(lax.ppermute(send, 'dp', ring))  28.6 us
    ppermute x8, starting transfers between devices, body(): returned.append(lax.ppermute(piece, ('expert', 'dp'), pairs))  21.7 us
    ppermute x6, waiting for transfers between devices, exchange(): lax.ppermute(messages[t], 'expert', [(q, q ^ t) for q in range(experts)])  20.8 us
    all_to_all x2, waiting for transfers between devices, exchange(): lax.all_to_all(blocks, 'dp', split_axis=0, concat_axis=0, tiled=True)  15.1 us
    pallas_call x2, Pallas kernels, gradients(): pl.pallas_call(functools.partial(gradients_kernel, units, scale, grads is...  11.2 us
    pallas_call x4, Pallas kernels, back_rows(): pl.pallas_call(back_kernel, out_shape=jax.ShapeDtypeStruct((size, slots,...  11.2 us
    pallas_call x1, Pallas kernels, gate_up(): pl.pallas_call(gate_up_kernel, out_shape=(out, out, jax.ShapeDtypeStruct(...  10.7 us
  transfers between devices with their start and end apart: 43, of which 25 were waited for; matrix products, arithmetic and copies ran while one was open for 0% of the time, Pallas kernels for 20%

profile of v1, /device:TPU:0, one launch (start us, length us, event | category | flops | bytes accessed | tf_op | source)
XLA Modules:
  0.0 215.0 jit_solution(7028920558557228334)
XLA Ops:
  3.4 3.0 %collective-permute-start = (bf16[2,64,896]{2,1,0:T(8,128)(2,1)S(1)}, bf16[2,64,896]{2,1,0:T(8,128)(2,1)S(1)}, u32[]{:S(2)}, u32[]{:S(2)}) collective-permute-start(bf16[2,64,896]{2,1,0:T(8,128)(2,1)S(1)} %get-tuple-element.38), channel_id=1, source_target_pairs={{0,8},{8,0},{16,24},{24,16},{1,9},{9,1},{17,25},{25,17},{2,10},{10... | collective-permute-start | bytes 688136 | tf_op jit(solution)/shard_map/ppermute | solution.py:543
  7.9 4.9 %collective-permute-done.refs_1_ = bf16[2,64,896]{2,1,0:T(8,128)(2,1)S(1)} collective-permute-done((bf16[2,64,896]{2,1,0:T(8,128)(2,1)S(1)}, bf16[2,64,896]{2,1,0:T(8,128)(2,1)S(1)}, u32[]{:S(2)}, u32[]{:S(2)}) %collective-permute-start) | collective-permute-done | bytes 229408 | tf_op jit(solution)/shard_map/ppermute | solution.py:543
  12.8 5.5 %collective-permute-done.1.refs_2_ = bf16[2,64,896]{2,1,0:T(8,128)(2,1)S(1)} collective-permute-done((bf16[2,64,896]{2,1,0:T(8,128)(2,1)S(1)}, bf16[2,64,896]{2,1,0:T(8,128)(2,1)S(1)}, u32[]{:S(2)}, u32[]{:S(2)}) %collective-permute-start.1) | collective-permute-done | bytes 229408 | tf_op jit(solution)/shard_map/ppermute | solution.py:543
  18.4 2.7 %shard_map.103 = bf16[4,2,64,896]{3,2,1,0:T(8,128)(2,1)} custom-call(s32[21]{0:T(128)S(1)} %stack.87.scalar_ref, bf16[2,64,896]{2,1,0:T(8,128)(2,1)S(1)} %get-tuple-element.37.refs_0_, bf16[2,64,896]{2,1,0:T(8,128)(2,1)S(1)} %collective-permute-done.refs_1_, bf16[2,64,896]{2,1,0:T(8,128)(2,1)S(1)} %collective-permute-done.1.refs_2_, ...), custom_call_target="tpu_custom_call" | custom-call | flops 1024 | bytes 1024 | tf_op jit(solution)/shard_map/pallas_call | solution.py:131
  21.1 4.9 %all-to-all-start = ((bf16[8,64,896]{2,1,0:T(8,128)(2,1)}), bf16[8,64,896]{2,1,0:T(8,128)(2,1)S(1)}, u32[]{:S(2)}, u32[]{:S(2)}) async-start(bf16[8,64,896]{2,1,0:T(8,128)(2,1)} %bitcast.23), calls=%async_computation | async-start | bytes 1835008 | tf_op jit(solution)/shard_map/all_to_all | solution.py:545
  32.0 4.9 %collective-permute-done.3.refs_1_ = bf16[2,64,896]{2,1,0:T(8,128)(2,1)S(1)} collective-permute-done((bf16[2,64,896]{2,1,0:T(8,128)(2,1)S(1)}, bf16[2,64,896]{2,1,0:T(8,128)(2,1)S(1)}, u32[]{:S(2)}, u32[]{:S(2)}) %collective-permute-start.3) | collective-permute-done | bytes 229408 | tf_op jit(solution)/shard_map/ppermute | solution.py:543
  36.9 3.9 %collective-permute-done.4.refs_2_ = bf16[2,64,896]{2,1,0:T(8,128)(2,1)S(1)} collective-permute-done((bf16[2,64,896]{2,1,0:T(8,128)(2,1)S(1)}, bf16[2,64,896]{2,1,0:T(8,128)(2,1)S(1)}, u32[]{:S(2)}, u32[]{:S(2)}) %collective-permute-start.4) | collective-permute-done | bytes 229408 | tf_op jit(solution)/shard_map/ppermute | solution.py:543
  42.4 2.7 %shard_map.106 = bf16[4,2,64,896]{3,2,1,0:T(8,128)(2,1)} custom-call(s32[21]{0:T(128)S(1)} %stack.87.scalar_ref, bf16[2,64,896]{2,1,0:T(8,128)(2,1)S(1)} %get-tuple-element.43.refs_0_, bf16[2,64,896]{2,1,0:T(8,128)(2,1)S(1)} %collective-permute-done.3.refs_1_, bf16[2,64,896]{2,1,0:T(8,128)(2,1)S(1)} %collective-permute-done.4.refs_2_, ...), custom_call_target="tpu_custom_call" | custom-call | flops 1024 | bytes 1024 | tf_op jit(solution)/shard_map/pallas_call | solution.py:131
  45.1 4.6 %all-to-all-done = bf16[8,64,896]{2,1,0:T(8,128)(2,1)S(1)} async-done(((bf16[8,64,896]{2,1,0:T(8,128)(2,1)}), bf16[8,64,896]{2,1,0:T(8,128)(2,1)S(1)}, u32[]{:S(2)}, u32[]{:S(2)}) %all-to-all-start) | async-done | bytes 917536 | tf_op jit(solution)/shard_map/all_to_all | solution.py:545
  49.8 3.6 %all-to-all-start.1 = ((bf16[8,64,896]{2,1,0:T(8,128)(2,1)}), bf16[8,64,896]{2,1,0:T(8,128)(2,1)S(1)}, u32[]{:S(2)}, u32[]{:S(2)}) async-start(bf16[8,64,896]{2,1,0:T(8,128)(2,1)} %bitcast.27), calls=%async_computation.1 | async-start | bytes 1835008 | tf_op jit(solution)/shard_map/all_to_all | solution.py:545
  54.5 10.7 %shard_map.104 = (bf16[4,512,512]{2,1,0:T(8,128)(2,1)}, bf16[4,512,512]{2,1,0:T(8,128)(2,1)S(1)}, bf16[896,512]{1,0:T(8,128)(2,1)S(1)}) custom-call(s32[21]{0:T(128)S(1)} %stack.87.scalar_ref, bf16[512,896]{1,0:T(8,128)(2,1)S(1)} %bitcast.39, bf16[896,2048]{1,0:T(8,128)(2,1)} %bitcast.40, bf16[896,2048]{1,0:T(8,128)(2,1)} %bitcast.49), custom_call_target="tpu_custom_call" | custom-call | flops 1024 | bytes 1024 | tf_op jit(solution)/shard_map/pallas_call | solution.py:229
  66.5 10.5 %all-to-all-done.1 = bf16[8,64,896]{2,1,0:T(8,128)(2,1)S(1)} async-done(((bf16[8,64,896]{2,1,0:T(8,128)(2,1)}), bf16[8,64,896]{2,1,0:T(8,128)(2,1)S(1)}, u32[]{:S(2)}, u32[]{:S(2)}) %all-to-all-start.1) | async-done | bytes 917536 | tf_op jit(solution)/shard_map/all_to_all | solution.py:545
  81.5 3.1 %shard_map.108.refs_0_.refs_1_ = bf16[2,512,768]{2,1,0:T(8,128)(2,1)S(1)} custom-call(s32[21]{0:T(128)S(1)} %stack.87.scalar_ref, bf16[512,896]{1,0:T(8,128)(2,1)S(1)} %bitcast.34, bf16[2048,896]{1,0:T(8,128)(2,1)} %bitcast.59, bf16[2,512,256]{2,1,0:T(8,128)(2,1)S(1)} %collective-permute-done.6.refs_0_, bf16[4,512,512]{2,1,0:T(8,128)(2,1)S(1)} %get-tuple-element.47.refs_1_, ...), custom_call_target="tpu_custom_call" | custom-call | flops 1024 | bytes 1024 | tf_op jit(solution)/shard_map/pallas_call | solution.py:272
  96.8 3.1 %shard_map.112.refs_1_ = bf16[2,512,768]{2,1,0:T(8,128)(2,1)S(1)} custom-call(s32[21]{0:T(128)S(1)} %stack.87.scalar_ref, bf16[512,896]{1,0:T(8,128)(2,1)S(1)} %bitcast.36, bf16[2048,896]{1,0:T(8,128)(2,1)} %bitcast.61, bf16[2,512,256]{2,1,0:T(8,128)(2,1)S(1)} %collective-permute-done.10.refs_0_, bf16[4,512,512]{2,1,0:T(8,128)(2,1)S(1)} %get-tuple-element.47.refs_1_, ...), custom_call_target="tpu_custom_call" | custom-call | flops 1024 | bytes 1024 | tf_op jit(solution)/shard_map/pallas_call | solution.py:272
  115.3 2.6 %collective-permute-start.17 = (bf16[256,768]{1,0:T(8,128)(2,1)S(1)}, bf16[256,768]{1,0:T(8,128)(2,1)S(1)}, u32[]{:S(2)}, u32[]{:S(2)}) collective-permute-start(bf16[256,768]{1,0:T(8,128)(2,1)S(1)} %shard_map.119), channel_id=1, source_target_pairs={{0,2},{2,4},{4,6},{6,7},{7,5},{5,3},{3,1},{1,0},{8,10},{10,12},{12... | collective-permute-start | bytes 1179656 | tf_op jit(solution)/shard_map/ppermute | solution.py:577
  119.5 2.6 %collective-permute-start.18 = (bf16[256,768]{1,0:T(8,128)(2,1)S(1)}, bf16[256,768]{1,0:T(8,128)(2,1)S(1)}, u32[]{:S(2)}, u32[]{:S(2)}) collective-permute-start(bf16[256,768]{1,0:T(8,128)(2,1)S(1)} %shard_map.120), channel_id=1, source_target_pairs={{0,2},{2,4},{4,6},{6,7},{7,5},{5,3},{3,1},{1,0},{8,10},{10,12},{12... | collective-permute-start | bytes 1179656 | tf_op jit(solution)/shard_map/ppermute | solution.py:577
  166.1 4.6 %shard_map.126 = (bf16[896,2048]{1,0:T(8,128)(2,1)}, bf16[896,2048]{1,0:T(8,128)(2,1)}, bf16[2048,896]{1,0:T(8,128)(2,1)}, s32[21]{0:T(128)S(1)}) custom-call(s32[21]{0:T(128)S(1)} %stack.87.scalar_ref, bf16[896,512]{1,0:T(8,128)(2,1)S(1)} %copy-done.3, bf16[512,896]{1,0:T(8,128)(2,1)S(1)} %bitcast.37, bf16[512,768]{1,0:T(8,128)(2,1)S(1)} %get-tuple-element.49.refs_0_, ...), custom_call_target="tpu_custom_call" | custom-call | flops 1024 | bytes 1024 | tf_op jit(solution)/shard_map/pallas_call | solution.py:429
  172.5 4.1 %shard_map.128 = (f32[512,896]{1,0:T(8,128)S(1)}, s32[21]{0:T(128)}) custom-call(s32[21]{0:T(128)S(1)} %get-tuple-element.52.scalar_ref, bf16[512,768]{1,0:T(8,128)(2,1)S(1)} %get-tuple-element.49.refs_0_, bf16[512,768]{1,0:T(8,128)(2,1)S(1)} %get-tuple-element.50.refs_1_, bf16[512,768]{1,0:T(8,128)(2,1)S(1)} %get-tuple-element.51.refs_2_, ...), custom_call_target="tpu_custom_call" | custom-call | flops 1024 | bytes 1024 | tf_op jit(solution)/shard_map/pallas_call | solution.py:497
  176.7 5.9 %shard_map.129 = (bf16[64,896]{1,0:T(8,128)(2,1)S(1)}, bf16[64,896]{1,0:T(8,128)(2,1)S(1)}, bf16[64,896]{1,0:T(8,128)(2,1)S(1)}, bf16[64,896]{1,0:T(8,128)(2,1)S...) custom-call(s32[21]{0:T(128)S(1)} %stack.87.scalar_ref, ...), custom_call_target="tpu_custom_call" | custom-call | flops 1024 | bytes 1024 | tf_op jit(solution)/shard_map/pallas_call | solution.py:497
  183.3 2.9 %collective-permute-start.34 = (bf16[64,896]{1,0:T(8,128)(2,1)S(1)}, bf16[64,896]{1,0:T(8,128)(2,1)S(1)}, u32[]{:S(2)}, u32[]{:S(2)}) collective-permute-start(bf16[64,896]{1,0:T(8,128)(2,1)S(1)} %get-tuple-element.55), channel_id=1, source_target_pairs={{8,0},{0,1},{24,2},{16,3},{9,4},{1,5},{25,6},{17,7},{10,8},{2,9},{... | collective-permute-start | bytes 344072 | tf_op jit(solution)/shard_map/ppermute | solution.py:601
  188.6 5.0 %collective-permute-start.36 = (bf16[64,896]{1,0:T(8,128)(2,1)S(1)}, bf16[64,896]{1,0:T(8,128)(2,1)S(1)}, u32[]{:S(2)}, u32[]{:S(2)}) collective-permute-start(bf16[64,896]{1,0:T(8,128)(2,1)S(1)} %get-tuple-element.57), channel_id=1, source_target_pairs={{24,0},{16,1},{8,2},{0,3},{25,4},{17,5},{9,6},{1,7},{26,8},{18,9},... | collective-permute-start | bytes 344072 | tf_op jit(solution)/shard_map/ppermute | solution.py:601
  195.0 5.0 %collective-permute-start.38 = (bf16[64,896]{1,0:T(8,128)(2,1)S(1)}, bf16[64,896]{1,0:T(8,128)(2,1)S(1)}, u32[]{:S(2)}, u32[]{:S(2)}) collective-permute-start(bf16[64,896]{1,0:T(8,128)(2,1)S(1)} %get-tuple-element.59), channel_id=1, source_target_pairs={{9,0},{1,1},{25,2},{17,3},{8,4},{0,5},{24,6},{16,7},{11,8},{3,9},{... | collective-permute-start | bytes 344072 | tf_op jit(solution)/shard_map/ppermute | solution.py:601
  204.4 6.6 %shard_map.131 = (bf16[896,2048]{1,0:T(8,128)(2,1)}, bf16[896,2048]{1,0:T(8,128)(2,1)}, bf16[2048,896]{1,0:T(8,128)(2,1)}, s32[21]{0:T(128)}) custom-call(s32[21]{0:T(128)S(1)} %stack.87.scalar_ref, bf16[896,512]{1,0:T(8,128)(2,1)S(1)} %copy-done.3, bf16[512,896]{1,0:T(8,128)(2,1)S(1)} %bitcast.38, ...), custom_call_target="tpu_custom_call", output_to_operand_aliasing={{0}: (8, {}), {1}: (9, {}), {2}: (10, {})} | custom-call | flops 1024 | bytes 1024 | tf_op jit(solution)/shard_map/pallas_call | solution.py:429
  211.9 2.9 %shard_map.130 = bf16[128,1792]{1,0:T(8,128)(2,1)} custom-call(s32[21]{0:T(128)S(1)} %stack.87.scalar_ref, bf16[256,128]{1,0:T(8,128)(2,1)S(1)} %get-tuple-element.36.hot_ref, bf16[64,896]{1,0:T(8,128)(2,1)} %copy-done.4, bf16[64,896]{1,0:T(8,128)(2,1)} %copy-done.5, bf16[64,896]{1,0:T(8,128)(2,1)} %copy-done.6, bf16[64,896]{1,0:T(8,128)(2,1)} %copy-done.7, ...), custom_call_target="tpu_custom_call" | custom-call | flops 1024 | bytes 1024 | tf_op jit(solution)/shard_map/pallas_call | solution.py:184
  (117 shorter events, 103.3 us)
Async XLA Ops:
  3.4 9.4 %collective-permute-start = (bf16[2,64,896]{2,1,0:T(8,128)(2,1)S(1)}, bf16[2,64,896]{2,1,0:T(8,128)(2,1)S(1)}, u32[]{:S(2)}, u32[]{:S(2)}) collective-permute-start(bf16[2,64,896]{2,1,0:T(8,128)(2,1)S(1)} %get-tuple-element.38), channel_id=1, source_target_pairs={{0,8},{8,0},{16,24},{24,16},{1,9},{9,1},{17,25},{25,17},{2,10},{10... | collective-permute-start | bytes 688136 | tf_op jit(solution)/shard_map/ppermute | solution.py:543
  6.4 12.0 %collective-permute-start.1 = (bf16[2,64,896]{2,1,0:T(8,128)(2,1)S(1)}, bf16[2,64,896]{2,1,0:T(8,128)(2,1)S(1)}, u32[]{:S(2)}, u32[]{:S(2)}) collective-permute-start(bf16[2,64,896]{2,1,0:T(8,128)(2,1)S(1)} %get-tuple-element.39), channel_id=1, source_target_pairs={{0,16},{8,24},{16,0},{24,8},{1,17},{9,25},{17,1},{25,9},{2,18},{10... | collective-permute-start | bytes 688136 | tf_op jit(solution)/shard_map/ppermute | solution.py:543
  7.9 10.5 %collective-permute-start.2 = (bf16[2,64,896]{2,1,0:T(8,128)(2,1)S(1)}, bf16[2,64,896]{2,1,0:T(8,128)(2,1)S(1)}, u32[]{:S(2)}, u32[]{:S(2)}) collective-permute-start(bf16[2,64,896]{2,1,0:T(8,128)(2,1)S(1)} %get-tuple-element.40), channel_id=1, source_target_pairs={{0,24},{8,16},{16,8},{24,0},{1,25},{9,17},{17,9},{25,1},{2,26},{10... | collective-permute-start | bytes 688136 | tf_op jit(solution)/shard_map/ppermute | solution.py:543
  21.1 28.7 %all-to-all-start = ((bf16[8,64,896]{2,1,0:T(8,128)(2,1)}), bf16[8,64,896]{2,1,0:T(8,128)(2,1)S(1)}, u32[]{:S(2)}, u32[]{:S(2)}) async-start(bf16[8,64,896]{2,1,0:T(8,128)(2,1)} %bitcast.23), calls=%async_computation | async-start | bytes 1835008 | tf_op jit(solution)/shard_map/all_to_all | solution.py:545
  29.8 11.0 %collective-permute-start.4 = (bf16[2,64,896]{2,1,0:T(8,128)(2,1)S(1)}, bf16[2,64,896]{2,1,0:T(8,128)(2,1)S(1)}, u32[]{:S(2)}, u32[]{:S(2)}) collective-permute-start(bf16[2,64,896]{2,1,0:T(8,128)(2,1)S(1)} %get-tuple-element.45), channel_id=1, source_target_pairs={{0,16},{8,24},{16,0},{24,8},{1,17},{9,25},{17,1},{25,9},{2,18},{10... | collective-permute-start | bytes 688136 | tf_op jit(solution)/shard_map/ppermute | solution.py:543
  30.6 11.8 %collective-permute-start.5 = (bf16[2,64,896]{2,1,0:T(8,128)(2,1)S(1)}, bf16[2,64,896]{2,1,0:T(8,128)(2,1)S(1)}, u32[]{:S(2)}, u32[]{:S(2)}) collective-permute-start(bf16[2,64,896]{2,1,0:T(8,128)(2,1)S(1)} %get-tuple-element.46), channel_id=1, source_target_pairs={{0,24},{8,16},{16,8},{24,0},{1,25},{9,17},{17,9},{25,1},{2,26},{10... | collective-permute-start | bytes 688136 | tf_op jit(solution)/shard_map/ppermute | solution.py:543
  49.8 27.3 %all-to-all-start.1 = ((bf16[8,64,896]{2,1,0:T(8,128)(2,1)}), bf16[8,64,896]{2,1,0:T(8,128)(2,1)S(1)}, u32[]{:S(2)}, u32[]{:S(2)}) async-start(bf16[8,64,896]{2,1,0:T(8,128)(2,1)} %bitcast.27), calls=%async_computation.1 | async-start | bytes 1835008 | tf_op jit(solution)/shard_map/all_to_all | solution.py:545
  66.1 15.4 %collective-permute-start.7 = (bf16[4,512,512]{2,1,0:T(8,128)(2,1)}, bf16[4,512,512]{2,1,0:T(8,128)(2,1)}, u32[]{:S(2)}, u32[]{:S(2)}) collective-permute-start(bf16[4,512,512]{2,1,0:T(8,128)(2,1)} %get-tuple-element.48), channel_id=1, source_target_pairs={{0,1},{1,0},{2,3},{3,2},{4,5},{5,4},{6,7},{7,6},{8,9},{9,8},{10,11... | collective-permute-start | bytes 6291464 | tf_op jit(solution)/shard_map/ppermute | solution.py:554
  84.7 9.5 %collective-permute-start.13 = (bf16[256,768]{1,0:T(8,128)(2,1)S(1)}, bf16[256,768]{1,0:T(8,128)(2,1)S(1)}, u32[]{:S(2)}, u32[]{:S(2)}) collective-permute-start(bf16[256,768]{1,0:T(8,128)(2,1)S(1)} %shard_map.115), channel_id=1, source_target_pairs={{0,2},{2,4},{4,6},{6,7},{7,5},{5,3},{3,1},{1,0},{8,10},{10,12},{12... | collective-permute-start | bytes 1179656 | tf_op jit(solution)/shard_map/ppermute | solution.py:577
  87.4 9.4 %collective-permute-start.10 = (bf16[2,512,256]{2,1,0:T(8,128)(2,1)S(1)}, bf16[2,512,256]{2,1,0:T(8,128)(2,1)S(1)}, u32[]{:S(2)}, u32[]{:S(2)}) collective-permute-start(bf16[2,512,256]{2,1,0:T(8,128)(2,1)S(1)} %shard_map.111), channel_id=1, source_target_pairs={{0,1},{1,0},{2,3},{3,2},{4,5},{5,4},{6,7},{7,6},{8,9},{9,8},{10,11... | collective-permute-start | bytes 1572872 | tf_op jit(solution)/shard_map/ppermute | solution.py:557
  90.1 9.8 %collective-permute-start.9 = (bf16[256,768]{1,0:T(8,128)(2,1)S(1)}, bf16[256,768]{1,0:T(8,128)(2,1)S(1)}, u32[]{:S(2)}, u32[]{:S(2)}) collective-permute-start(bf16[256,768]{1,0:T(8,128)(2,1)S(1)} %shard_map.110), channel_id=1, source_target_pairs={{0,2},{2,4},{4,6},{6,7},{7,5},{5,3},{3,1},{1,0},{8,10},{10,12},{12... | collective-permute-start | bytes 1179656 | tf_op jit(solution)/shard_map/ppermute | solution.py:577
  157.4 13.3 %collective-permute-start.27 = (bf16[256,768]{1,0:T(8,128)(2,1)S(1)}, bf16[256,768]{1,0:T(8,128)(2,1)S(1)}, u32[]{:S(2)}, u32[]{:S(2)}) collective-permute-start(bf16[256,768]{1,0:T(8,128)(2,1)S(1)} %collective-permute-done.25.refs_10_.refs_4_), channel_id=1, source_target_pairs={{0,2},{2,4},{4,6},{6,7},{7,5},{5,3},{3,1},{1,0},{8,10},{10,12},{12... | collective-permute-start | bytes 1179656 | tf_op jit(solution)/shard_map/ppermute | solution.py:577
  161.6 9.1 %collective-permute-start.28 = (bf16[256,768]{1,0:T(8,128)(2,1)S(1)}, bf16[256,768]{1,0:T(8,128)(2,1)S(1)}, u32[]{:S(2)}, u32[]{:S(2)}) collective-permute-start(bf16[256,768]{1,0:T(8,128)(2,1)S(1)} %collective-permute-done.26.refs_11_.refs_5_), channel_id=1, source_target_pairs={{0,2},{2,4},{4,6},{6,7},{7,5},{5,3},{3,1},{1,0},{8,10},{10,12},{12... | collective-permute-start | bytes 1179656 | tf_op jit(solution)/shard_map/ppermute | solution.py:577
  165.5 11.2 %collective-permute-start.29 = (bf16[512,768]{1,0:T(8,128)(2,1)S(1)}, bf16[512,768]{1,0:T(8,128)(2,1)S(1)}, u32[]{:S(2)}, u32[]{:S(2)}) collective-permute-start(bf16[512,768]{1,0:T(8,128)(2,1)S(1)} %get-tuple-element.49.refs_0_), channel_id=1, source_target_pairs={{0,1},{1,0},{2,3},{3,2},{4,5},{5,4},{6,7},{7,6},{8,9},{9,8},{10,11... | collective-permute-start | bytes 2359304 | tf_op jit(solution)/shard_map/ppermute | solution.py:586
  165.6 11.1 %collective-permute-start.30 = (bf16[512,768]{1,0:T(8,128)(2,1)S(1)}, bf16[512,768]{1,0:T(8,128)(2,1)S(1)}, u32[]{:S(2)}, u32[]{:S(2)}) collective-permute-start(bf16[512,768]{1,0:T(8,128)(2,1)S(1)} %get-tuple-element.50.refs_1_), channel_id=1, source_target_pairs={{0,1},{1,0},{2,3},{3,2},{4,5},{5,4},{6,7},{7,6},{8,9},{9,8},{10,11... | collective-permute-start | bytes 2359304 | tf_op jit(solution)/shard_map/ppermute | solution.py:586
  166.1 10.6 %collective-permute-start.31 = (bf16[512,768]{1,0:T(8,128)(2,1)S(1)}, bf16[512,768]{1,0:T(8,128)(2,1)S(1)}, u32[]{:S(2)}, u32[]{:S(2)}) collective-permute-start(bf16[512,768]{1,0:T(8,128)(2,1)S(1)} %get-tuple-element.51.refs_2_), channel_id=1, source_target_pairs={{0,1},{1,0},{2,3},{3,2},{4,5},{5,4},{6,7},{7,6},{8,9},{9,8},{10,11... | collective-permute-start | bytes 2359304 | tf_op jit(solution)/shard_map/ppermute | solution.py:586
  182.6 12.4 %collective-permute-start.33 = (bf16[64,896]{1,0:T(8,128)(2,1)S(1)}, bf16[64,896]{1,0:T(8,128)(2,1)S(1)}, u32[]{:S(2)}, u32[]{:S(2)}) collective-permute-start(bf16[64,896]{1,0:T(8,128)(2,1)S(1)} %get-tuple-element.54), channel_id=1, source_target_pairs={{0,0},{8,1},{16,2},{24,3},{1,4},{9,5},{17,6},{25,7},{2,8},{10,9},{... | collective-permute-start | bytes 344072 | tf_op jit(solution)/shard_map/ppermute | solution.py:601
  183.3 16.7 %collective-permute-start.34 = (bf16[64,896]{1,0:T(8,128)(2,1)S(1)}, bf16[64,896]{1,0:T(8,128)(2,1)S(1)}, u32[]{:S(2)}, u32[]{:S(2)}) collective-permute-start(bf16[64,896]{1,0:T(8,128)(2,1)S(1)} %get-tuple-element.55), channel_id=1, source_target_pairs={{8,0},{0,1},{24,2},{16,3},{9,4},{1,5},{25,6},{17,7},{10,8},{2,9},{... | collective-permute-start | bytes 344072 | tf_op jit(solution)/shard_map/ppermute | solution.py:601
  186.2 15.8 %collective-permute-start.35 = (bf16[64,896]{1,0:T(8,128)(2,1)S(1)}, bf16[64,896]{1,0:T(8,128)(2,1)S(1)}, u32[]{:S(2)}, u32[]{:S(2)}) collective-permute-start(bf16[64,896]{1,0:T(8,128)(2,1)S(1)} %get-tuple-element.56), channel_id=1, source_target_pairs={{16,0},{24,1},{0,2},{8,3},{17,4},{25,5},{1,6},{9,7},{18,8},{26,9},... | collective-permute-start | bytes 344072 | tf_op jit(solution)/shard_map/ppermute | solution.py:601
  188.6 22.4 %collective-permute-start.36 = (bf16[64,896]{1,0:T(8,128)(2,1)S(1)}, bf16[64,896]{1,0:T(8,128)(2,1)S(1)}, u32[]{:S(2)}, u32[]{:S(2)}) collective-permute-start(bf16[64,896]{1,0:T(8,128)(2,1)S(1)} %get-tuple-element.57), channel_id=1, source_target_pairs={{24,0},{16,1},{8,2},{0,3},{25,4},{17,5},{9,6},{1,7},{26,8},{18,9},... | collective-permute-start | bytes 344072 | tf_op jit(solution)/shard_map/ppermute | solution.py:601
  193.6 17.5 %collective-permute-start.37 = (bf16[64,896]{1,0:T(8,128)(2,1)S(1)}, bf16[64,896]{1,0:T(8,128)(2,1)S(1)}, u32[]{:S(2)}, u32[]{:S(2)}) collective-permute-start(bf16[64,896]{1,0:T(8,128)(2,1)S(1)} %get-tuple-element.58), channel_id=1, source_target_pairs={{1,0},{9,1},{17,2},{25,3},{0,4},{8,5},{16,6},{24,7},{3,8},{11,9},{... | collective-permute-start | bytes 344072 | tf_op jit(solution)/shard_map/ppermute | solution.py:601
  195.0 16.1 %collective-permute-start.38 = (bf16[64,896]{1,0:T(8,128)(2,1)S(1)}, bf16[64,896]{1,0:T(8,128)(2,1)S(1)}, u32[]{:S(2)}, u32[]{:S(2)}) collective-permute-start(bf16[64,896]{1,0:T(8,128)(2,1)S(1)} %get-tuple-element.59), channel_id=1, source_target_pairs={{9,0},{1,1},{25,2},{17,3},{8,4},{0,5},{24,6},{16,7},{11,8},{3,9},{... | collective-permute-start | bytes 344072 | tf_op jit(solution)/shard_map/ppermute | solution.py:601
  200.0 11.1 %collective-permute-start.39 = (bf16[64,896]{1,0:T(8,128)(2,1)S(1)}, bf16[64,896]{1,0:T(8,128)(2,1)S(1)}, u32[]{:S(2)}, u32[]{:S(2)}) collective-permute-start(bf16[64,896]{1,0:T(8,128)(2,1)S(1)} %get-tuple-element.60), channel_id=1, source_target_pairs={{17,0},{25,1},{1,2},{9,3},{16,4},{24,5},{0,6},{8,7},{19,8},{27,9},... | collective-permute-start | bytes 344072 | tf_op jit(solution)/shard_map/ppermute | solution.py:601
  202.0 9.1 %collective-permute-start.40 = (bf16[64,896]{1,0:T(8,128)(2,1)S(1)}, bf16[64,896]{1,0:T(8,128)(2,1)S(1)}, u32[]{:S(2)}, u32[]{:S(2)}) collective-permute-start(bf16[64,896]{1,0:T(8,128)(2,1)S(1)} %get-tuple-element.61), channel_id=1, source_target_pairs={{25,0},{17,1},{9,2},{1,3},{24,4},{16,5},{8,6},{0,7},{27,8},{19,9},... | collective-permute-start | bytes 344072 | tf_op jit(solution)/shard_map/ppermute | solution.py:601
  (31 other events, 224.0 us)

commit v2 on v1

--- a/solution.py
+++ b/solution.py
@@ -203,45 +203,57 @@
     return out
 
 
-def gate_up_kernel(scalar_ref, x_ref, wg_ref, wu_ref, *outs):
+def gate_up_kernel(count, scalar_ref, x_ref, wg_ref, wu_ref, *outs):
+    others, (own_ref, turned_ref) = outs[:count], outs[count:]
     width = wg_ref.shape[1]
-
-    @pl.when((pl.program_id(0) == 0) & (pl.program_id(1) == 0))
+    chunk, own = pl.program_id(0), pl.program_id(1)
+
+    @pl.when((chunk == 0) & (own == 0))
     def _():
-        outs[2][...] = x_ref[...].T
-
-    for own in range(2):
-
-        @pl.when(pl.program_id(1) == own)
+        turned_ref[...] = x_ref[...].T
+
+    def write(out_ref):
+        out_ref[0, :, :width] = dot(x_ref[...], wg_ref[...]).astype(BF16)
+        out_ref[0, :, width:] = dot(x_ref[...], wu_ref[...]).astype(BF16)
+
+    @pl.when(own == 1)
+    def _():
+        write(own_ref)
+
+    for n, out_ref in enumerate(others):
+
+        @pl.when((own == 0) & (chunk == n))
         def _():
-            outs[own][0, :, :width] = dot(x_ref[...], wg_ref[...]).astype(BF16)
-            outs[own][0, :, width:] = dot(x_ref[...], wu_ref[...]).astype(BF16)
+            write(out_ref)
 
 
 def gate_up(scalars, x, w_gate, w_up, count):
     slots, feats = x.shape
     width = w_gate.shape[1] // (2 * count)
-    out = jax.ShapeDtypeStruct((count, slots, 2 * width), BF16)
-    out_spec = pl.BlockSpec((1, slots, 2 * width), lambda i, own, c: (i, 0, 0))
     column = pl.BlockSpec(
         (feats, width), lambda i, own, c: (0, c[FIXED + 2 * count + own * count + i])
     )
-    return pl.pallas_call(
-        gate_up_kernel,
-        out_shape=(out, out, jax.ShapeDtypeStruct((feats, slots), BF16)),
+    *others, own, turned = pl.pallas_call(
+        functools.partial(gate_up_kernel, count),
+        out_shape=[jax.ShapeDtypeStruct((1, slots, 2 * width), BF16)] * count
+        + [
+            jax.ShapeDtypeStruct((count, slots, 2 * width), BF16),
+            jax.ShapeDtypeStruct((feats, slots), BF16),
+        ],
         grid_spec=pltpu.PrefetchScalarGridSpec(
             num_scalar_prefetch=1,
             grid=(count, 2),
             in_specs=[pl.BlockSpec((slots, feats), lambda i, own, c: (0, 0)), column, column],
-            out_specs=(
-                out_spec,
-                out_spec,
+            out_specs=[pl.BlockSpec((1, slots, 2 * width), lambda i, own, c: (0, 0, 0))] * count
+            + [
+                pl.BlockSpec((1, slots, 2 * width), lambda i, own, c: (i, 0, 0)),
                 pl.BlockSpec((feats, slots), lambda i, own, c: (0, 0)),
-            ),
+            ],
         ),
         compiler_params=PARAMS,
         cost_estimate=cost(),
     )(scalars, x, *in_hbm(w_gate, w_up))
+    return others, own, turned
 
 
 def back_kernel(scalar_ref, g_ref, wd_ref, *refs):
@@ -267,7 +279,8 @@
     in_specs = [pl.BlockSpec((slots, feats), lambda i, c: (0, 0)), row]
     if own:
         in_specs.append(pl.BlockSpec((1, slots, width), lambda i, c: (i, 0, 0)))
-        in_specs += [pl.BlockSpec((1, slots, 2 * width), lambda i, c: (begin + i, 0, 0))] * 2
+        in_specs.append(pl.BlockSpec((1, slots, 2 * width), lambda i, c: (begin + i, 0, 0)))
+        in_specs.append(pl.BlockSpec((1, slots, 2 * width), lambda i, c: (0, 0, 0)))
     cols = (3 if own else 1) * width
     return pl.pallas_call(
         back_kernel,
@@ -551,17 +564,15 @@
     g = exchange(g_messages)
 
     other_gu, own_gu, x_t = gate_up(scalars, x, w_gate, w_up, count)
-    sib_gu = lax.ppermute(other_gu, "dp", swap)
-    spans = ((0, count // 2), (count // 2, count - count // 2))
-    others = [
-        lax.ppermute(back_rows(scalars, g, w_down, begin, size, count, ()), "dp", swap)
-        for begin, size in spans
-    ]
     sums = []
-    for (begin, size), sib_b in zip(spans, others):
-        shares = (sib_b, own_gu, sib_gu)
-        both = back_rows(scalars, g, w_down, begin, size, count, shares)
-        sums += [(both, i) for i in range(size)]
+    for i in range(count):
+        other_b = back_rows(scalars, g, w_down, i, 1, count, ())
+        shares = (
+            lax.ppermute(other_b, "dp", swap),
+            own_gu,
+            lax.ppermute(other_gu[i], "dp", swap),
+        )
+        sums.append((back_rows(scalars, g, w_down, i, 1, count, shares), 0))
 
     slots = 2 * count + chips - 2
     first_back = chips - 1 + count

time: 216 us -> 217 us (level)
  waiting for transfers between devices: 66.4 us -> 60.8 us
  Pallas kernels: 59.8 us -> 65.1 us
  local copies, waits for them, and re-layouts: 2.95 us -> 6.02 us
    ppermute x20, waiting for transfers between devices: 28.6 us -> 22.2 us  [body(): came.append(lax.ppermute(send, 'dp', ring))]
    pallas_call x4 -> x8, Pallas kernels: 11.2 us -> 16.9 us  [back_rows(): pl.pallas_call(back_kernel, out_shape=jax.ShapeDtypeStruct((size, slots,...]
    ppermute x20, starting transfers between devices: 43.7 us -> 40.4 us  [body(): came.append(lax.ppermute(send, 'dp', ring))]
    unnamed x24 -> x40, local copies, waits for them, and re-layouts: 2.85 us -> 5.92 us
    ppermute x3 -> x8, waiting for transfers between devices: 1.9 us -> 4.61 us  [the longest x4 4.6 us: body(): lax.ppermute(other_b, 'dp', swap)]
  transfers between devices with their start and end apart: 43 -> 48, of which waited for: 25 -> 25; matrix products, arithmetic and copies ran while one was open for 0% -> 0% of each run, Pallas kernels for 20% -> 24%
where the time goes in v2:
time: 217 us; the launch traced here: 216 us
  starting transfers between devices  82.2 us (38%)
  Pallas kernels  65.1 us (30%)
  waiting for transfers between devices  60.8 us (28%)
  local copies, waits for them, and re-layouts  6.02 us (3%)
    ppermute x20, starting transfers between devices, body(): came.append(lax.ppermute(send, 'dp', ring))  40.4 us
    ppermute x20, waiting for transfers between devices, body(): came.append(lax.ppermute(send, 'dp', ring))  22.2 us
    ppermute x8, starting transfers between devices, body(): returned.append(lax.ppermute(piece, ('expert', 'dp'), pairs))  22 us
    ppermute x6, waiting for transfers between devices, exchange(): lax.ppermute(messages[t], 'expert', [(q, q ^ t) for q in range(experts)])  20.9 us
    pallas_call x8, Pallas kernels, back_rows(): pl.pallas_call(back_kernel, out_shape=jax.ShapeDtypeStruct((size, slots,...  16.9 us
    all_to_all x2, waiting for transfers between devices, exchange(): lax.all_to_all(blocks, 'dp', split_axis=0, concat_axis=0, tiled=True)  13.1 us
    pallas_call x2, Pallas kernels, gradients(): pl.pallas_call(functools.partial(gradients_kernel, units, scale, grads is...  11.2 us
    pallas_call x1, Pallas kernels, gate_up(): pl.pallas_call(functools.partial(gate_up_kernel, count), out_shape=[jax.S...  10.3 us
  transfers between devices with their start and end apart: 48, of which 25 were waited for; matrix products, arithmetic and copies ran while one was open for 0% of the time, Pallas kernels for 24%

profile of v2, /device:TPU:0, one launch (start us, length us, event | category | flops | bytes accessed | tf_op | source)
XLA Modules:
  0.0 215.6 jit_solution(12142322284200126875)
XLA Ops:
  4.0 2.9 %collective-permute-start = (bf16[2,64,896]{2,1,0:T(8,128)(2,1)S(1)}, bf16[2,64,896]{2,1,0:T(8,128)(2,1)S(1)}, u32[]{:S(2)}, u32[]{:S(2)}) collective-permute-start(bf16[2,64,896]{2,1,0:T(8,128)(2,1)S(1)} %get-tuple-element.41), channel_id=1, source_target_pairs={{0,8},{8,0},{16,24},{24,16},{1,9},{9,1},{17,25},{25,17},{2,10},{10... | collective-permute-start | bytes 688136 | tf_op jit(solution)/shard_map/ppermute | solution.py:556
  8.5 4.9 %collective-permute-done.refs_1_ = bf16[2,64,896]{2,1,0:T(8,128)(2,1)S(1)} collective-permute-done((bf16[2,64,896]{2,1,0:T(8,128)(2,1)S(1)}, bf16[2,64,896]{2,1,0:T(8,128)(2,1)S(1)}, u32[]{:S(2)}, u32[]{:S(2)}) %collective-permute-start) | collective-permute-done | bytes 229408 | tf_op jit(solution)/shard_map/ppermute | solution.py:556
  13.4 5.5 %collective-permute-done.1.refs_2_ = bf16[2,64,896]{2,1,0:T(8,128)(2,1)S(1)} collective-permute-done((bf16[2,64,896]{2,1,0:T(8,128)(2,1)S(1)}, bf16[2,64,896]{2,1,0:T(8,128)(2,1)S(1)}, u32[]{:S(2)}, u32[]{:S(2)}) %collective-permute-start.1) | collective-permute-done | bytes 229408 | tf_op jit(solution)/shard_map/ppermute | solution.py:556
  18.9 2.7 %shard_map.103 = bf16[4,2,64,896]{3,2,1,0:T(8,128)(2,1)} custom-call(s32[21]{0:T(128)S(1)} %stack.87.scalar_ref, bf16[2,64,896]{2,1,0:T(8,128)(2,1)S(1)} %get-tuple-element.40.refs_0_, bf16[2,64,896]{2,1,0:T(8,128)(2,1)S(1)} %collective-permute-done.refs_1_, bf16[2,64,896]{2,1,0:T(8,128)(2,1)S(1)} %collective-permute-done.1.refs_2_, ...), custom_call_target="tpu_custom_call" | custom-call | flops 1024 | bytes 1024 | tf_op jit(solution)/shard_map/pallas_call | solution.py:131
  21.6 4.9 %all-to-all-start = ((bf16[8,64,896]{2,1,0:T(8,128)(2,1)}), bf16[8,64,896]{2,1,0:T(8,128)(2,1)S(1)}, u32[]{:S(2)}, u32[]{:S(2)}) async-start(bf16[8,64,896]{2,1,0:T(8,128)(2,1)} %bitcast.23), calls=%async_computation | async-start | bytes 1835008 | tf_op jit(solution)/shard_map/all_to_all | solution.py:558
  32.6 4.9 %collective-permute-done.3.refs_1_ = bf16[2,64,896]{2,1,0:T(8,128)(2,1)S(1)} collective-permute-done((bf16[2,64,896]{2,1,0:T(8,128)(2,1)S(1)}, bf16[2,64,896]{2,1,0:T(8,128)(2,1)S(1)}, u32[]{:S(2)}, u32[]{:S(2)}) %collective-permute-start.3) | collective-permute-done | bytes 229408 | tf_op jit(solution)/shard_map/ppermute | solution.py:556
  37.5 3.9 %collective-permute-done.4.refs_2_ = bf16[2,64,896]{2,1,0:T(8,128)(2,1)S(1)} collective-permute-done((bf16[2,64,896]{2,1,0:T(8,128)(2,1)S(1)}, bf16[2,64,896]{2,1,0:T(8,128)(2,1)S(1)}, u32[]{:S(2)}, u32[]{:S(2)}) %collective-permute-start.4) | collective-permute-done | bytes 229408 | tf_op jit(solution)/shard_map/ppermute | solution.py:556
  43.0 2.7 %shard_map.106 = bf16[4,2,64,896]{3,2,1,0:T(8,128)(2,1)} custom-call(s32[21]{0:T(128)S(1)} %stack.87.scalar_ref, bf16[2,64,896]{2,1,0:T(8,128)(2,1)S(1)} %get-tuple-element.46.refs_0_, bf16[2,64,896]{2,1,0:T(8,128)(2,1)S(1)} %collective-permute-done.3.refs_1_, bf16[2,64,896]{2,1,0:T(8,128)(2,1)S(1)} %collective-permute-done.4.refs_2_, ...), custom_call_target="tpu_custom_call" | custom-call | flops 1024 | bytes 1024 | tf_op jit(solution)/shard_map/pallas_call | solution.py:131
  45.7 4.6 %all-to-all-done = bf16[8,64,896]{2,1,0:T(8,128)(2,1)S(1)} async-done(((bf16[8,64,896]{2,1,0:T(8,128)(2,1)}), bf16[8,64,896]{2,1,0:T(8,128)(2,1)S(1)}, u32[]{:S(2)}, u32[]{:S(2)}) %all-to-all-start) | async-done | bytes 917536 | tf_op jit(solution)/shard_map/all_to_all | solution.py:558
  50.3 3.6 %all-to-all-start.1 = ((bf16[8,64,896]{2,1,0:T(8,128)(2,1)}), bf16[8,64,896]{2,1,0:T(8,128)(2,1)S(1)}, u32[]{:S(2)}, u32[]{:S(2)}) async-start(bf16[8,64,896]{2,1,0:T(8,128)(2,1)} %bitcast.27), calls=%async_computation.1 | async-start | bytes 1835008 | tf_op jit(solution)/shard_map/all_to_all | solution.py:558
  55.1 10.3 %shard_map.104 = (bf16[1,512,512]{2,1,0:T(8,128)(2,1)}, bf16[1,512,512]{2,1,0:T(8,128)(2,1)S(1)}, bf16[1,512,512]{2,1,0:T(8,128)(2,1)S(1)}, bf16[1,512,512]{2,1,...) custom-call(s32[21]{0:T(128)S(1)} %stack.87.scalar_ref, ...), custom_call_target="tpu_custom_call" | custom-call | flops 1024 | bytes 1024 | tf_op jit(solution)/shard_map/pallas_call | solution.py:236
  69.1 8.5 %all-to-all-done.1 = bf16[8,64,896]{2,1,0:T(8,128)(2,1)S(1)} async-done(((bf16[8,64,896]{2,1,0:T(8,128)(2,1)}), bf16[8,64,896]{2,1,0:T(8,128)(2,1)S(1)}, u32[]{:S(2)}, u32[]{:S(2)}) %all-to-all-start.1) | async-done | bytes 917536 | tf_op jit(solution)/shard_map/all_to_all | solution.py:558
  116.3 2.6 %collective-permute-start.22 = (bf16[256,768]{1,0:T(8,128)(2,1)S(1)}, bf16[256,768]{1,0:T(8,128)(2,1)S(1)}, u32[]{:S(2)}, u32[]{:S(2)}) collective-permute-start(bf16[256,768]{1,0:T(8,128)(2,1)S(1)} %shard_map.123), channel_id=1, source_target_pairs={{0,2},{2,4},{4,6},{6,7},{7,5},{5,3},{3,1},{1,0},{8,10},{10,12},{12... | collective-permute-start | bytes 1179656 | tf_op jit(solution)/shard_map/ppermute | solution.py:588
  120.3 2.6 %collective-permute-start.23 = (bf16[256,768]{1,0:T(8,128)(2,1)S(1)}, bf16[256,768]{1,0:T(8,128)(2,1)S(1)}, u32[]{:S(2)}, u32[]{:S(2)}) collective-permute-start(bf16[256,768]{1,0:T(8,128)(2,1)S(1)} %shard_map.124), channel_id=1, source_target_pairs={{0,2},{2,4},{4,6},{6,7},{7,5},{5,3},{3,1},{1,0},{8,10},{10,12},{12... | collective-permute-start | bytes 1179656 | tf_op jit(solution)/shard_map/ppermute | solution.py:588
  166.8 4.6 %shard_map.130 = (bf16[896,2048]{1,0:T(8,128)(2,1)}, bf16[896,2048]{1,0:T(8,128)(2,1)}, bf16[2048,896]{1,0:T(8,128)(2,1)}, s32[21]{0:T(128)S(1)}) custom-call(s32[21]{0:T(128)S(1)} %stack.87.scalar_ref, bf16[896,512]{1,0:T(8,128)(2,1)S(1)} %copy-done.3, bf16[512,896]{1,0:T(8,128)(2,1)S(1)} %bitcast.41, bf16[512,768]{1,0:T(8,128)(2,1)S(1)} %get-tuple-element.55.refs_0_, ...), custom_call_target="tpu_custom_call" | custom-call | flops 1024 | bytes 1024 | tf_op jit(solution)/shard_map/pallas_call | solution.py:442
  172.9 4.2 %shard_map.132 = (f32[512,896]{1,0:T(8,128)S(1)}, s32[21]{0:T(128)}) custom-call(s32[21]{0:T(128)S(1)} %get-tuple-element.58.scalar_ref, bf16[512,768]{1,0:T(8,128)(2,1)S(1)} %get-tuple-element.55.refs_0_, bf16[512,768]{1,0:T(8,128)(2,1)S(1)} %get-tuple-element.56.refs_1_, bf16[512,768]{1,0:T(8,128)(2,1)S(1)} %get-tuple-element.57.refs_2_, ...), custom_call_target="tpu_custom_call" | custom-call | flops 1024 | bytes 1024 | tf_op jit(solution)/shard_map/pallas_call | solution.py:510
  177.1 5.9 %shard_map.133 = (bf16[64,896]{1,0:T(8,128)(2,1)S(1)}, bf16[64,896]{1,0:T(8,128)(2,1)S(1)}, bf16[64,896]{1,0:T(8,128)(2,1)S(1)}, bf16[64,896]{1,0:T(8,128)(2,1)S...) custom-call(s32[21]{0:T(128)S(1)} %stack.87.scalar_ref, ...), custom_call_target="tpu_custom_call" | custom-call | flops 1024 | bytes 1024 | tf_op jit(solution)/shard_map/pallas_call | solution.py:510
  183.7 3.9 %collective-permute-start.39 = (bf16[64,896]{1,0:T(8,128)(2,1)S(1)}, bf16[64,896]{1,0:T(8,128)(2,1)S(1)}, u32[]{:S(2)}, u32[]{:S(2)}) collective-permute-start(bf16[64,896]{1,0:T(8,128)(2,1)S(1)} %get-tuple-element.61), channel_id=1, source_target_pairs={{8,0},{0,1},{24,2},{16,3},{9,4},{1,5},{25,6},{17,7},{10,8},{2,9},{... | collective-permute-start | bytes 344072 | tf_op jit(solution)/shard_map/ppermute | solution.py:612
  187.6 2.6 %collective-permute-start.40 = (bf16[64,896]{1,0:T(8,128)(2,1)S(1)}, bf16[64,896]{1,0:T(8,128)(2,1)S(1)}, u32[]{:S(2)}, u32[]{:S(2)}) collective-permute-start(bf16[64,896]{1,0:T(8,128)(2,1)S(1)} %get-tuple-element.62), channel_id=1, source_target_pairs={{16,0},{24,1},{0,2},{8,3},{17,4},{25,5},{1,6},{9,7},{18,8},{26,9},... | collective-permute-start | bytes 344072 | tf_op jit(solution)/shard_map/ppermute | solution.py:612
  190.2 4.2 %collective-permute-start.41 = (bf16[64,896]{1,0:T(8,128)(2,1)S(1)}, bf16[64,896]{1,0:T(8,128)(2,1)S(1)}, u32[]{:S(2)}, u32[]{:S(2)}) collective-permute-start(bf16[64,896]{1,0:T(8,128)(2,1)S(1)} %get-tuple-element.63), channel_id=1, source_target_pairs={{24,0},{16,1},{8,2},{0,3},{25,4},{17,5},{9,6},{1,7},{26,8},{18,9},... | collective-permute-start | bytes 344072 | tf_op jit(solution)/shard_map/ppermute | solution.py:612
  195.8 4.3 %collective-permute-start.43 = (bf16[64,896]{1,0:T(8,128)(2,1)S(1)}, bf16[64,896]{1,0:T(8,128)(2,1)S(1)}, u32[]{:S(2)}, u32[]{:S(2)}) collective-permute-start(bf16[64,896]{1,0:T(8,128)(2,1)S(1)} %get-tuple-element.65), channel_id=1, source_target_pairs={{9,0},{1,1},{25,2},{17,3},{8,4},{0,5},{24,6},{16,7},{11,8},{3,9},{... | collective-permute-start | bytes 344072 | tf_op jit(solution)/shard_map/ppermute | solution.py:612
  202.1 2.9 %collective-permute-start.45 = (bf16[64,896]{1,0:T(8,128)(2,1)S(1)}, bf16[64,896]{1,0:T(8,128)(2,1)S(1)}, u32[]{:S(2)}, u32[]{:S(2)}) collective-permute-start(bf16[64,896]{1,0:T(8,128)(2,1)S(1)} %get-tuple-element.67), channel_id=1, source_target_pairs={{25,0},{17,1},{9,2},{1,3},{24,4},{16,5},{8,6},{0,7},{27,8},{19,9},... | collective-permute-start | bytes 344072 | tf_op jit(solution)/shard_map/ppermute | solution.py:612
  205.0 6.6 %shard_map.135 = (bf16[896,2048]{1,0:T(8,128)(2,1)}, bf16[896,2048]{1,0:T(8,128)(2,1)}, bf16[2048,896]{1,0:T(8,128)(2,1)}, s32[21]{0:T(128)}) custom-call(s32[21]{0:T(128)S(1)} %stack.87.scalar_ref, bf16[896,512]{1,0:T(8,128)(2,1)S(1)} %copy-done.3, bf16[512,896]{1,0:T(8,128)(2,1)S(1)} %bitcast.42, ...), custom_call_target="tpu_custom_call", output_to_operand_aliasing={{0}: (8, {}), {1}: (9, {}), {2}: (10, {})} | custom-call | flops 1024 | bytes 1024 | tf_op jit(solution)/shard_map/pallas_call | solution.py:442
  212.5 2.9 %shard_map.134 = bf16[128,1792]{1,0:T(8,128)(2,1)} custom-call(s32[21]{0:T(128)S(1)} %stack.87.scalar_ref, bf16[256,128]{1,0:T(8,128)(2,1)S(1)} %copy-done.5, bf16[64,896]{1,0:T(8,128)(2,1)} %copy-done.12, bf16[64,896]{1,0:T(8,128)(2,1)} %copy-done.13, bf16[64,896]{1,0:T(8,128)(2,1)} %copy-done.14, bf16[64,896]{1,0:T(8,128)(2,1)} %copy-done.15, ...), custom_call_target="tpu_custom_call" | custom-call | flops 1024 | bytes 1024 | tf_op jit(solution)/shard_map/pallas_call | solution.py:184
  (147 shorter events, 107.3 us)
Async XLA Ops:
  7.0 12.0 %collective-permute-start.1 = (bf16[2,64,896]{2,1,0:T(8,128)(2,1)S(1)}, bf16[2,64,896]{2,1,0:T(8,128)(2,1)S(1)}, u32[]{:S(2)}, u32[]{:S(2)}) collective-permute-start(bf16[2,64,896]{2,1,0:T(8,128)(2,1)S(1)} %get-tuple-element.42), channel_id=1, source_target_pairs={{0,16},{8,24},{16,0},{24,8},{1,17},{9,25},{17,1},{25,9},{2,18},{10... | collective-permute-start | bytes 688136 | tf_op jit(solution)/shard_map/ppermute | solution.py:556
  8.5 10.5 %collective-permute-start.2 = (bf16[2,64,896]{2,1,0:T(8,128)(2,1)S(1)}, bf16[2,64,896]{2,1,0:T(8,128)(2,1)S(1)}, u32[]{:S(2)}, u32[]{:S(2)}) collective-permute-start(bf16[2,64,896]{2,1,0:T(8,128)(2,1)S(1)} %get-tuple-element.43), channel_id=1, source_target_pairs={{0,24},{8,16},{16,8},{24,0},{1,25},{9,17},{17,9},{25,1},{2,26},{10... | collective-permute-start | bytes 688136 | tf_op jit(solution)/shard_map/ppermute | solution.py:556
  21.6 28.7 %all-to-all-start = ((bf16[8,64,896]{2,1,0:T(8,128)(2,1)}), bf16[8,64,896]{2,1,0:T(8,128)(2,1)S(1)}, u32[]{:S(2)}, u32[]{:S(2)}) async-start(bf16[8,64,896]{2,1,0:T(8,128)(2,1)} %bitcast.23), calls=%async_computation | async-start | bytes 1835008 | tf_op jit(solution)/shard_map/all_to_all | solution.py:558
  30.3 11.0 %collective-permute-start.4 = (bf16[2,64,896]{2,1,0:T(8,128)(2,1)S(1)}, bf16[2,64,896]{2,1,0:T(8,128)(2,1)S(1)}, u32[]{:S(2)}, u32[]{:S(2)}) collective-permute-start(bf16[2,64,896]{2,1,0:T(8,128)(2,1)S(1)} %get-tuple-element.48), channel_id=1, source_target_pairs={{0,16},{8,24},{16,0},{24,8},{1,17},{9,25},{17,1},{25,9},{2,18},{10... | collective-permute-start | bytes 688136 | tf_op jit(solution)/shard_map/ppermute | solution.py:556
  31.2 11.8 %collective-permute-start.5 = (bf16[2,64,896]{2,1,0:T(8,128)(2,1)S(1)}, bf16[2,64,896]{2,1,0:T(8,128)(2,1)S(1)}, u32[]{:S(2)}, u32[]{:S(2)}) collective-permute-start(bf16[2,64,896]{2,1,0:T(8,128)(2,1)S(1)} %get-tuple-element.49), channel_id=1, source_target_pairs={{0,24},{8,16},{16,8},{24,0},{1,25},{9,17},{17,9},{25,1},{2,26},{10... | collective-permute-start | bytes 688136 | tf_op jit(solution)/shard_map/ppermute | solution.py:556
  50.3 27.3 %all-to-all-start.1 = ((bf16[8,64,896]{2,1,0:T(8,128)(2,1)}), bf16[8,64,896]{2,1,0:T(8,128)(2,1)S(1)}, u32[]{:S(2)}, u32[]{:S(2)}) async-start(bf16[8,64,896]{2,1,0:T(8,128)(2,1)} %bitcast.27), calls=%async_computation.1 | async-start | bytes 1835008 | tf_op jit(solution)/shard_map/all_to_all | solution.py:558
  68.7 12.5 %collective-permute-start.7 = (bf16[1,512,512]{2,1,0:T(8,128)(2,1)}, bf16[1,512,512]{2,1,0:T(8,128)(2,1)S(1)}, u32[]{:S(2)}, u32[]{:S(2)}) collective-permute-start(bf16[1,512,512]{2,1,0:T(8,128)(2,1)} %get-tuple-element.51), channel_id=1, source_target_pairs={{0,1},{1,0},{2,3},{3,2},{4,5},{5,4},{6,7},{7,6},{8,9},{9,8},{10,11... | collective-permute-start | bytes 1572872 | tf_op jit(solution)/shard_map/ppermute | solution.py:573
  83.6 9.5 %collective-permute-start.18 = (bf16[256,768]{1,0:T(8,128)(2,1)S(1)}, bf16[256,768]{1,0:T(8,128)(2,1)S(1)}, u32[]{:S(2)}, u32[]{:S(2)}) collective-permute-start(bf16[256,768]{1,0:T(8,128)(2,1)S(1)} %shard_map.119), channel_id=1, source_target_pairs={{0,2},{2,4},{4,6},{6,7},{7,5},{5,3},{3,1},{1,0},{8,10},{10,12},{12... | collective-permute-start | bytes 1179656 | tf_op jit(solution)/shard_map/ppermute | solution.py:588
  86.2 13.1 %collective-permute-start.13 = (bf16[1,512,512]{2,1,0:T(8,128)(2,1)S(1)}, bf16[1,512,512]{2,1,0:T(8,128)(2,1)S(1)}, u32[]{:S(2)}, u32[]{:S(2)}) collective-permute-start(bf16[1,512,512]{2,1,0:T(8,128)(2,1)S(1)} %copy-done.9), channel_id=1, source_target_pairs={{0,1},{1,0},{2,3},{3,2},{4,5},{5,4},{6,7},{7,6},{8,9},{9,8},{10,11... | collective-permute-start | bytes 1572872 | tf_op jit(solution)/shard_map/ppermute | solution.py:573
  89.7 11.8 %collective-permute-start.11 = (bf16[256,768]{1,0:T(8,128)(2,1)S(1)}, bf16[256,768]{1,0:T(8,128)(2,1)S(1)}, u32[]{:S(2)}, u32[]{:S(2)}) collective-permute-start(bf16[256,768]{1,0:T(8,128)(2,1)S(1)} %shard_map.112), channel_id=1, source_target_pairs={{0,2},{2,4},{4,6},{6,7},{7,5},{5,3},{3,1},{1,0},{8,10},{10,12},{12... | collective-permute-start | bytes 1179656 | tf_op jit(solution)/shard_map/ppermute | solution.py:588
  97.8 10.0 %collective-permute-start.16 = (bf16[1,512,512]{2,1,0:T(8,128)(2,1)S(1)}, bf16[1,512,512]{2,1,0:T(8,128)(2,1)S(1)}, u32[]{:S(2)}, u32[]{:S(2)}) collective-permute-start(bf16[1,512,512]{2,1,0:T(8,128)(2,1)S(1)} %copy-done.7), channel_id=1, source_target_pairs={{0,1},{1,0},{2,3},{3,2},{4,5},{5,4},{6,7},{7,6},{8,9},{9,8},{10,11... | collective-permute-start | bytes 1572872 | tf_op jit(solution)/shard_map/ppermute | solution.py:573
  102.0 9.4 %collective-permute-start.20 = (bf16[256,768]{1,0:T(8,128)(2,1)S(1)}, bf16[256,768]{1,0:T(8,128)(2,1)S(1)}, u32[]{:S(2)}, u32[]{:S(2)}) collective-permute-start(bf16[256,768]{1,0:T(8,128)(2,1)S(1)} %shard_map.121), channel_id=1, source_target_pairs={{0,2},{2,4},{4,6},{6,7},{7,5},{5,3},{3,1},{1,0},{8,10},{10,12},{12... | collective-permute-start | bytes 1179656 | tf_op jit(solution)/shard_map/ppermute | solution.py:588
  158.2 13.2 %collective-permute-start.32 = (bf16[256,768]{1,0:T(8,128)(2,1)S(1)}, bf16[256,768]{1,0:T(8,128)(2,1)S(1)}, u32[]{:S(2)}, u32[]{:S(2)}) collective-permute-start(bf16[256,768]{1,0:T(8,128)(2,1)S(1)} %collective-permute-done.30.refs_10_.refs_4_), channel_id=1, source_target_pairs={{0,2},{2,4},{4,6},{6,7},{7,5},{5,3},{3,1},{1,0},{8,10},{10,12},{12... | collective-permute-start | bytes 1179656 | tf_op jit(solution)/shard_map/ppermute | solution.py:588
  166.1 10.9 %collective-permute-start.34 = (bf16[512,768]{1,0:T(8,128)(2,1)S(1)}, bf16[512,768]{1,0:T(8,128)(2,1)S(1)}, u32[]{:S(2)}, u32[]{:S(2)}) collective-permute-start(bf16[512,768]{1,0:T(8,128)(2,1)S(1)} %get-tuple-element.55.refs_0_), channel_id=1, source_target_pairs={{0,1},{1,0},{2,3},{3,2},{4,5},{5,4},{6,7},{7,6},{8,9},{9,8},{10,11... | collective-permute-start | bytes 2359304 | tf_op jit(solution)/shard_map/ppermute | solution.py:597
  166.2 10.8 %collective-permute-start.35 = (bf16[512,768]{1,0:T(8,128)(2,1)S(1)}, bf16[512,768]{1,0:T(8,128)(2,1)S(1)}, u32[]{:S(2)}, u32[]{:S(2)}) collective-permute-start(bf16[512,768]{1,0:T(8,128)(2,1)S(1)} %get-tuple-element.56.refs_1_), channel_id=1, source_target_pairs={{0,1},{1,0},{2,3},{3,2},{4,5},{5,4},{6,7},{7,6},{8,9},{9,8},{10,11... | collective-permute-start | bytes 2359304 | tf_op jit(solution)/shard_map/ppermute | solution.py:597
  166.7 10.3 %collective-permute-start.36 = (bf16[512,768]{1,0:T(8,128)(2,1)S(1)}, bf16[512,768]{1,0:T(8,128)(2,1)S(1)}, u32[]{:S(2)}, u32[]{:S(2)}) collective-permute-start(bf16[512,768]{1,0:T(8,128)(2,1)S(1)} %get-tuple-element.57.refs_2_), channel_id=1, source_target_pairs={{0,1},{1,0},{2,3},{3,2},{4,5},{5,4},{6,7},{7,6},{8,9},{9,8},{10,11... | collective-permute-start | bytes 2359304 | tf_op jit(solution)/shard_map/ppermute | solution.py:597
  183.0 12.8 %collective-permute-start.38 = (bf16[64,896]{1,0:T(8,128)(2,1)S(1)}, bf16[64,896]{1,0:T(8,128)(2,1)S(1)}, u32[]{:S(2)}, u32[]{:S(2)}) collective-permute-start(bf16[64,896]{1,0:T(8,128)(2,1)S(1)} %get-tuple-element.60), channel_id=1, source_target_pairs={{0,0},{8,1},{16,2},{24,3},{1,4},{9,5},{17,6},{25,7},{2,8},{10,9},{... | collective-permute-start | bytes 344072 | tf_op jit(solution)/shard_map/ppermute | solution.py:612
  183.7 16.5 %collective-permute-start.39 = (bf16[64,896]{1,0:T(8,128)(2,1)S(1)}, bf16[64,896]{1,0:T(8,128)(2,1)S(1)}, u32[]{:S(2)}, u32[]{:S(2)}) collective-permute-start(bf16[64,896]{1,0:T(8,128)(2,1)S(1)} %get-tuple-element.61), channel_id=1, source_target_pairs={{8,0},{0,1},{24,2},{16,3},{9,4},{1,5},{25,6},{17,7},{10,8},{2,9},{... | collective-permute-start | bytes 344072 | tf_op jit(solution)/shard_map/ppermute | solution.py:612
  187.6 14.5 %collective-permute-start.40 = (bf16[64,896]{1,0:T(8,128)(2,1)S(1)}, bf16[64,896]{1,0:T(8,128)(2,1)S(1)}, u32[]{:S(2)}, u32[]{:S(2)}) collective-permute-start(bf16[64,896]{1,0:T(8,128)(2,1)S(1)} %get-tuple-element.62), channel_id=1, source_target_pairs={{16,0},{24,1},{0,2},{8,3},{17,4},{25,5},{1,6},{9,7},{18,8},{26,9},... | collective-permute-start | bytes 344072 | tf_op jit(solution)/shard_map/ppermute | solution.py:612
  190.2 21.5 %collective-permute-start.41 = (bf16[64,896]{1,0:T(8,128)(2,1)S(1)}, bf16[64,896]{1,0:T(8,128)(2,1)S(1)}, u32[]{:S(2)}, u32[]{:S(2)}) collective-permute-start(bf16[64,896]{1,0:T(8,128)(2,1)S(1)} %get-tuple-element.63), channel_id=1, source_target_pairs={{24,0},{16,1},{8,2},{0,3},{25,4},{17,5},{9,6},{1,7},{26,8},{18,9},... | collective-permute-start | bytes 344072 | tf_op jit(solution)/shard_map/ppermute | solution.py:612
  194.4 17.3 %collective-permute-start.42 = (bf16[64,896]{1,0:T(8,128)(2,1)S(1)}, bf16[64,896]{1,0:T(8,128)(2,1)S(1)}, u32[]{:S(2)}, u32[]{:S(2)}) collective-permute-start(bf16[64,896]{1,0:T(8,128)(2,1)S(1)} %get-tuple-element.64), channel_id=1, source_target_pairs={{1,0},{9,1},{17,2},{25,3},{0,4},{8,5},{16,6},{24,7},{3,8},{11,9},{... | collective-permute-start | bytes 344072 | tf_op jit(solution)/shard_map/ppermute | solution.py:612
  195.8 15.8 %collective-permute-start.43 = (bf16[64,896]{1,0:T(8,128)(2,1)S(1)}, bf16[64,896]{1,0:T(8,128)(2,1)S(1)}, u32[]{:S(2)}, u32[]{:S(2)}) collective-permute-start(bf16[64,896]{1,0:T(8,128)(2,1)S(1)} %get-tuple-element.65), channel_id=1, source_target_pairs={{9,0},{1,1},{25,2},{17,3},{8,4},{0,5},{24,6},{16,7},{11,8},{3,9},{... | collective-permute-start | bytes 344072 | tf_op jit(solution)/shard_map/ppermute | solution.py:612
  200.2 11.5 %collective-permute-start.44 = (bf16[64,896]{1,0:T(8,128)(2,1)S(1)}, bf16[64,896]{1,0:T(8,128)(2,1)S(1)}, u32[]{:S(2)}, u32[]{:S(2)}) collective-permute-start(bf16[64,896]{1,0:T(8,128)(2,1)S(1)} %get-tuple-element.66), channel_id=1, source_target_pairs={{17,0},{25,1},{1,2},{9,3},{16,4},{24,5},{0,6},{8,7},{19,8},{27,9},... | collective-permute-start | bytes 344072 | tf_op jit(solution)/shard_map/ppermute | solution.py:612
  202.1 9.6 %collective-permute-start.45 = (bf16[64,896]{1,0:T(8,128)(2,1)S(1)}, bf16[64,896]{1,0:T(8,128)(2,1)S(1)}, u32[]{:S(2)}, u32[]{:S(2)}) collective-permute-start(bf16[64,896]{1,0:T(8,128)(2,1)S(1)} %get-tuple-element.67), channel_id=1, source_target_pairs={{25,0},{17,1},{9,2},{1,3},{24,4},{16,5},{8,6},{0,7},{27,8},{19,9},... | collective-permute-start | bytes 344072 | tf_op jit(solution)/shard_map/ppermute | solution.py:612
  (44 other events, 274.9 us)
